TPU v7x, 128 devices: a whole 4x4x4 slice. The times are simulated.
128 devices in a mesh: grp: 8 (over z, core), dev: 16 (over x, y).
Axes of the slice: x: 4, y: 4, z: 4, core: 2. Of those that a mesh axis runs over, the one named last changes fastest.
Arguments:
- probe_field: bfloat16 [896, 2, 16, 3584], P(('grp', 'dev')), may hold values from -6 to 6
- kappa_field: float32 [896, 2, 3584], P(('grp', 'dev')), may hold values from 0.5 to 2
- circle_order: int32 [896], replicated, may hold values from 0 to 895, each once
- pair_order: int32 [896], replicated, may hold values from 0 to 895, each once
- legendre_table: bfloat16 [896, 1793, 896], P(('grp', 'dev')), may hold values from -0.1875 to 0.1875
Outputs:
- filtered: bfloat16 [896, 2, 16, 3584], P(('grp', 'dev'))
Inputs may be any that keep to these rules, and one draw needn't show every extreme that they name: A permutation: latitude slot s holds latitude pair circle_order[s], whose side 0 is northern circle circle_order[s] and side 1 circle 1792 - 1-circle_order[s]. A permutation: table slot s holds wavenumbers q = pair_order[s] and 1791-q.
All inputs are finite; a program needn't handle non-finite values.
Results may differ from a plain program's by a relative error of at most 0.0083.
Values may be sent and summed in bfloat16 or wider, within the bound.
No kernel may reach another device: no remote copies, remote signals or barrier semaphores. Data moves between devices by JAX's collectives and lax.ppermute only.
A program may use at most 256 MiB of HBM per device.

v0:
```python
import math

import jax
import jax.numpy as jnp
from jax import lax
from jax.sharding import PartitionSpec as P


def wave_columns(pair_order, degrees):
    part_index = jnp.arange(4, dtype=jnp.int32)
    second = part_index >= 2
    wave_num = jnp.where(
        second[None, :], degrees - 1 - pair_order[:, None], pair_order[:, None]
    ).reshape(-1)
    imaginary = jnp.tile(part_index % 2, pair_order.shape[0])
    return (wave_num, imaginary)


def forward_table(pair_order, degrees, longitudes):
    wave_num, imaginary = wave_columns(pair_order, degrees)
    phase = jnp.arange(longitudes, dtype=jnp.int32)[:, None] * wave_num[None, :] % longitudes
    angle = phase.astype(jnp.float32) * (2.0 * math.pi / longitudes)
    values = jnp.where(imaginary[None, :] == 1, -jnp.sin(angle), jnp.cos(angle))
    return (values * longitudes ** (-0.5)).astype(jnp.bfloat16)


def inverse_table(pair_order, degrees, longitudes):
    wave_num, imaginary = wave_columns(pair_order, degrees)
    phase = wave_num[:, None] * jnp.arange(longitudes, dtype=jnp.int32)[None, :] % longitudes
    angle = phase.astype(jnp.float32) * (2.0 * math.pi / longitudes)
    values = jnp.where(imaginary[:, None] == 1, -jnp.sin(angle), jnp.cos(angle))
    weight = jnp.where(wave_num == 0, 1.0, 2.0).astype(jnp.float32)
    return (values * weight[:, None] * longitudes ** (-0.5)).astype(jnp.bfloat16)


def across_lat(rows, cols):
    return lax.dot_general(rows, cols, (((1,), (1,)), ((), ())), preferred_element_type=jnp.float32)


def across_deg(coef, rows):
    return lax.dot_general(coef, rows, (((0,), (0,)), ((), ())), preferred_element_type=jnp.float32)


def legendre(table_rows, blocks, pair_id):
    row_count, circle_half = table_rows.shape
    degrees = row_count - 1
    half = degrees // 2
    width = blocks.shape[2]
    flip = pair_id % 2
    upper = table_rows[:half].reshape(half // 2, 2, circle_half)
    lower = table_rows[half:degrees].reshape(half // 2, 2, circle_half)
    last_row = table_rows[degrees:]
    lower_index = half + 2 * jnp.arange(half // 2, dtype=jnp.int32)
    upper_parts = []
    lower_parts = []
    lower_second = []
    for side in range(2):
        upper_parts.append(across_lat(upper[:, side], blocks[side, 0]))
        other = jnp.where(flip == 0, blocks[side, 1], blocks[1 - side, 1])
        joined = jnp.concatenate([blocks[side, 0], other], axis=0)
        lower_prod = across_lat(lower[:, side], joined)
        second = lower_index + side >= degrees - pair_id
        lower_second.append(second)
        lower_parts.append(jnp.where(second[:, None], lower_prod[:, width:], lower_prod[:, :width]))
    last_cols = jnp.where(flip == 0, blocks[0, 1], blocks[1, 1])
    last_prod = across_lat(last_row, last_cols)
    spectrum = jnp.concatenate(
        [
            jnp.stack(upper_parts, axis=1).reshape(half, width),
            jnp.stack(lower_parts, axis=1).reshape(half, width),
            last_prod,
        ],
        axis=0,
    )
    row_index = jnp.arange(row_count, dtype=jnp.int32)
    second_all = row_index >= degrees - pair_id
    degree = jnp.where(second_all, row_index - 1, pair_id + row_index)
    degree_f = degree.astype(jnp.float32)
    damping = 1.0 / (1.0 + 4.0 * degree_f * (degree_f + 1.0) / float(degrees * degrees))
    scaled = (spectrum * damping[:, None]).astype(jnp.bfloat16)
    scaled_upper = scaled[:half].reshape(half // 2, 2, width)
    scaled_lower = scaled[half:degrees].reshape(half // 2, 2, width)
    scaled_last = scaled[degrees:]
    zero_block = jnp.zeros_like(scaled_lower[:, 0])
    first_sums = []
    second_sums = []
    for side in range(2):
        mask = lower_second[side][:, None]
        spread = jnp.concatenate(
            [
                jnp.where(mask, zero_block, scaled_lower[:, side]),
                jnp.where(mask, scaled_lower[:, side], zero_block),
            ],
            axis=1,
        )
        lower_out = across_deg(spread, lower[:, side])
        first_sums.append(across_deg(scaled_upper[:, side], upper[:, side]) + lower_out[:width])
        second_sums.append(lower_out[width:])
    last_out = across_deg(scaled_last, last_row)
    zero_out = jnp.zeros_like(last_out)
    second_even = jnp.where(flip == 0, second_sums[0], second_sums[1]) + jnp.where(
        flip == 0, last_out, zero_out
    )
    second_odd = jnp.where(flip == 0, second_sums[1], second_sums[0]) + jnp.where(
        flip == 0, zero_out, last_out
    )
    even_sum = jnp.stack([first_sums[0], second_even], axis=0)
    odd_sum = jnp.stack([first_sums[1], second_odd], axis=0)
    return jnp.stack([even_sum + odd_sum, even_sum - odd_sum], axis=0).astype(jnp.bfloat16)


def per_device(probe_field, kappa_field, circle_order, pair_order, legendre_table):
    circle_dev, hemispheres, probes, longitudes = probe_field.shape
    wave_dev, row_count, circle_half = legendre_table.shape
    degrees = row_count - 1
    devices = lax.axis_size(("grp", "dev"))
    weighted = (kappa_field[:, :, None, :] * probe_field.astype(jnp.float32)).astype(jnp.bfloat16)
    fourier = jnp.einsum(
        "lc,jhpl->chpj",
        forward_table(pair_order, degrees, longitudes),
        weighted,
        preferred_element_type=jnp.float32,
    ).astype(jnp.bfloat16)
    payload = fourier.reshape(devices, wave_dev, 4, hemispheres, probes, circle_dev)
    position = jnp.arange(circle_half, dtype=jnp.int32)
    back_select = (circle_order[:, None] == position[None, :]).astype(jnp.bfloat16)
    first_slot = lax.axis_index(("grp", "dev")) * wave_dev
    item_marks = jnp.broadcast_to(
        jnp.arange(wave_dev, dtype=jnp.float32).reshape(1, wave_dev, 1, 1, 1, 1),
        (devices, wave_dev, 1, 1, 1, 1),
    ).astype(jnp.bfloat16)
    received = lax.all_to_all(payload, ("grp", "dev"), split_axis=0, concat_axis=5, tiled=True)
    labels = lax.all_to_all(item_marks, ("grp", "dev"), split_axis=0, concat_axis=5, tiled=True)
    analyse_received = received[0]
    slot_ids = labels[0, :, 0, 0, 0, 0].astype(jnp.int32)
    natural = jnp.einsum(
        "iahpx,xj->iahpj", analyse_received, back_select, preferred_element_type=jnp.float32
    )
    north_circle = natural[:, :, 0]
    south_circle = natural[:, :, 1]
    columns = jnp.stack([north_circle + south_circle, north_circle - south_circle], axis=1).astype(
        jnp.bfloat16
    )
    item_count = columns.shape[0]
    columns = columns.reshape(item_count, 2, 2, 2 * probes, circle_half)
    slot_tables = jnp.take(legendre_table, slot_ids, axis=0)
    pair_ids = jnp.take(pair_order, first_slot + slot_ids)
    synthesis = jax.vmap(legendre)(slot_tables, columns, pair_ids)
    synthesis = synthesis.reshape(item_count, hemispheres, 4, probes, circle_half)
    answer = jnp.einsum(
        "ihapj,xj->ihapx", synthesis, back_select, preferred_element_type=jnp.float32
    ).astype(jnp.bfloat16)
    spectral = lax.all_to_all(answer[None], ("grp", "dev"), split_axis=5, concat_axis=0, tiled=True)
    backward = inverse_table(pair_order, degrees, longitudes).reshape(
        devices, wave_dev, 4, longitudes
    )
    values = jnp.einsum("swhapj,swal->jhpl", spectral, backward, preferred_element_type=jnp.float32)
    return (kappa_field[:, :, None, :] * values).astype(jnp.bfloat16)


def solution(mesh):
    return jax.shard_map(
        per_device,
        mesh=mesh,
        in_specs=(
            P(("grp", "dev"), None, None, None),
            P(("grp", "dev"), None, None),
            P(),
            P(),
            P(("grp", "dev"), None, None),
        ),
        out_specs=P(("grp", "dev"), None, None, None),
        check_vma=False,
    )
```

profile of v0, /device:TPU:1, one launch (start us, length us, event | category | flops | bytes accessed | tf_op | source)
XLA Modules:
  0.0 909.3 jit_solution(16799130307119374635)
XLA Ops:
  0.7 11.5 %all-to-all-start = ((bf16[128,7,1,1,1,1]{1,5,4,3,2,0:T(2,128)(2,1)}), bf16[128,7,1,1,1,1]{1,5,4,3,2,0:T(2,128)(2,1)S(1)}, u32[]{:S(2)}, u32[]{:S(2)}) async-start(bf16[128,7,1,1,1,1]{1,5,4,3,2,0:T(2,128)(2,1)} %broadcast_in_dim.185), calls=%async_computation | async-start | bytes 131072 | tf_op jit(solution)/shard_map/all_to_all | solution.py:133
  14.9 1.0 broadcast_select_fusion.2
  16.1 16.0 %fusion.107 = (bf16[7,896,896]{2,1,0:T(8,128)(2,1)}, bf16[7,896,896]{2,1,0:T(8,128)(2,1)}) fusion(bf16[7,1793,896]{2,1,0:T(8,128)(2,1)} %param.9), kind=kLoop, calls=%fused_computation.161 | loop fusion | bytes 44957696 | tf_op jit(solution)/shard_map/jit(_take)/gather | solution.py:146
  32.5 221.2 %fusion.33 = bf16[3584,2,16,7]{0,2,1,3:T(8,128)(2,1)S(1)} fusion(s32[3584]{0:T(1024)S(1)} %select_n.185, pred[3584]{0:T(1024)(128)(4,1)S(1)} %eq.67, bf16[7,2,16,3584]{3,2,1,0:T(8,128)(2,1)S(1)} %fusion.124), kind=kOutput, calls=%fused_computation.39 | convolution fusion | flops 5922373632 | bytes 3229184 | tf_op jit(solution)/shard_map/lc,jhpl->chpj/dot_general | solution.py:118
  254.7 8.3 copy.219
  263.0 9.8 %copy.310 = bf16[128,7,4,2,16,7]{4,2,1,5,3,0:T(4,128)(2,1)} copy(bf16[128,7,4,2,16,7]{4,2,1,0,5,3:T(4,128)(2,1)} %bitcast.195) | data formatting | bytes 3211264 | tf_op jit(solution)/shard_map/reshape | solution.py:124
  272.9 18.7 %reshape.576 = bf16[128,2,3136]{2,1,0:T(2,128)(2,1)} reshape(bf16[128,2,7,7,4,16]{5,4,3,2,1,0:T(4,128)(2,1)} %bitcast.196) | data formatting | bytes 3211264
  291.5 9.8 %all-to-all-start.1 = ((bf16[128,2,3136]{2,1,0:T(2,128)(2,1)}), bf16[128,2,3136]{2,1,0:T(2,128)(2,1)S(1)}, u32[]{:S(2)}, u32[]{:S(2)}) async-start(bf16[128,2,3136]{2,1,0:T(2,128)(2,1)} %reshape.576), calls=%async_computation.1 | async-start | bytes 3276800 | tf_op jit(solution)/shard_map/all_to_all | solution.py:132
  302.2 10.4 %gather_fusion.1 = bf16[7,896,896]{2,1,0:T(8,128)(2,1)} fusion(bf16[7,896,896]{2,1,0:T(8,128)(2,1)} %get-tuple-element.9, s32[1024]{0:T(1024)S(1)} %get-tuple-element.38), kind=kCustom, calls=%fused_computation.1 | custom fusion | bytes 22478876 | tf_op jit(solution)/shard_map/jit(_take)/gather | solution.py:146
  312.5 10.4 %gather_fusion.2 = bf16[7,896,896]{2,1,0:T(8,128)(2,1)} fusion(bf16[7,896,896]{2,1,0:T(8,128)(2,1)} %get-tuple-element.10, s32[1024]{0:T(1024)S(1)} %get-tuple-element.38), kind=kCustom, calls=%fused_computation.2 | custom fusion | bytes 22478876 | tf_op jit(solution)/shard_map/jit(_take)/gather | solution.py:146
  322.9 25.7 %maximum_select_fusion = bf16[7,1793,896]{2,1,0:T(8,128)(2,1)} fusion(bf16[7,1,896]{2,1,0:T(2,128)(2,1)S(1)} %copy.215, bf16[7,896,896]{2,1,0:T(8,128)(2,1)} %gather_fusion.2, bf16[7,896,896]{2,1,0:T(8,128)(2,1)} %gather_fusion.1, pred[7]{0:T(512)(128)(4,1)S(1)} %compare_and_fusion), kind=kLoop, calls=%fused_computation.26 | loop fusion | flops 78719872 | bytes 44982792 | tf_op jit(solution)/shard_map/jit(_take)/select_n | solution.py:146
  348.6 15.9 %fusion.106 = (bf16[7,896,896]{2,1,0:T(8,128)(2,1)}, bf16[7,896,896]{2,1,0:T(8,128)(2,1)}) fusion(bf16[7,1793,896]{2,1,0:T(8,128)(2,1)} %maximum_select_fusion), kind=kLoop, calls=%fused_computation.160 | loop fusion | bytes 44957696 | tf_op jit(solution)/shard_map/vmap()/slice | solution.py:50
  364.5 22.6 %reshape.520 = bf16[7,448,2,896]{3,2,1,0:T(2,128)(2,1)} reshape(bf16[7,896,896]{2,1,0:T(8,128)(2,1)} %get-tuple-element.7) | data formatting | bytes 22478848 | tf_op jit(solution)/shard_map/vmap()/reshape | solution.py:50
  387.1 22.6 %reshape.523 = bf16[7,448,2,896]{3,2,1,0:T(2,128)(2,1)} reshape(bf16[7,896,896]{2,1,0:T(8,128)(2,1)} %get-tuple-element.8) | data formatting | bytes 22478848 | tf_op jit(solution)/shard_map/vmap()/reshape | solution.py:51
  409.7 23.4 %fusion.109 = (bf16[7,448,1,896]{3,2,1,0:T(2,128)(2,1)}, bf16[7,448,1,896]{3,2,1,0:T(2,128)(2,1)}) fusion(bf16[7,448,2,896]{3,2,1,0:T(2,128)(2,1)} %reshape.523), kind=kLoop, calls=%fused_computation.163 | loop fusion | bytes 22478848 | tf_op jit(solution)/shard_map/vmap()/slice | solution.py:61
  433.1 17.4 %fusion.108 = (bf16[7,448,1,896]{3,2,1,0:T(2,128)(2,1)}, bf16[7,448,1,896]{3,2,1,0:T(2,128)(2,1)}) fusion(bf16[7,448,2,896]{3,2,1,0:T(2,128)(2,1)S(1)} %copy-done), kind=kLoop, calls=%fused_computation.162 | loop fusion | bytes 22478848 | tf_op jit(solution)/shard_map/vmap()/slice | solution.py:58
  452.3 10.7 %reshape.577 = bf16[128,2,7,7,4,16]{5,4,3,2,1,0:T(4,128)(2,1)} reshape(bf16[128,2,3136]{2,1,0:T(2,128)(2,1)S(1)} %all-to-all-done.1) | data formatting | bytes 3211264
  463.1 6.2 bitcast_bitcast_fusion
  469.2 15.5 %copy.221 = bf16[1,7,4,2,16,128,7]{4,3,6,5,2,1,0:T(2,128)(2,1)} copy(bf16[1,7,4,2,16,128,7]{4,2,1,6,3,5,0:T(4,128)(2,1)S(1)} %bitcast_bitcast_fusion) | data formatting | bytes 3211264 | tf_op jit(solution)/shard_map/all_to_all | solution.py:132
  484.7 8.8 fusion.18
  494.2 1.4 fusion.84
  495.6 6.1 fusion.45
  501.8 1.9 fusion.47
  503.8 1.0 pad_maximum_fusion.3
  504.8 4.5 copy.231
  509.3 6.0 fusion.62
  515.3 6.0 fusion.63
  521.3 1.0 pad_maximum_fusion.2
  522.3 5.7 copy.226
  528.0 4.4 fusion.20
  532.6 3.1 fusion.112
  535.7 4.2 copy.262
  542.5 3.1 fusion.111
  545.5 4.2 copy.261
  549.8 1.1 copy.264
  550.9 5.6 fusion.44
  556.5 5.4 fusion.46
  562.0 5.2 fusion.61
  567.2 1.0 fusion.59
  569.5 2.1 fusion.55
  571.6 18.1 %copy.238 = bf16[1,7,2,4,16,896]{4,3,2,1,0,5:T(4,128)(2,1)} copy(bf16[1,7,2,4,16,896]{5,4,3,2,1,0:T(8,128)(2,1)S(1)} %fusion.55) | data formatting | bytes 3211264 | tf_op jit(solution)/shard_map/broadcast_in_dim | solution.py:153
  589.7 18.7 %reshape.578 = bf16[128,2,3136]{2,1,0:T(2,128)(2,1)} reshape(bf16[896,1,7,2,4,16]{5,4,3,2,1,0:T(4,128)(2,1)} %bitcast.193) | data formatting | bytes 3211264
  608.4 10.1 %all-to-all-start.2 = ((bf16[128,2,3136]{2,1,0:T(2,128)(2,1)}), bf16[128,2,3136]{2,1,0:T(2,128)(2,1)S(1)}, u32[]{:S(2)}, u32[]{:S(2)}) async-start(bf16[128,2,3136]{2,1,0:T(2,128)(2,1)} %reshape.578), calls=%async_computation.2 | async-start | bytes 3276800 | tf_op jit(solution)/shard_map/all_to_all | solution.py:153
  619.2 24.0 %all-to-all-done.2 = bf16[128,2,3136]{2,1,0:T(2,128)(2,1)S(1)} async-done(((bf16[128,2,3136]{2,1,0:T(2,128)(2,1)}), bf16[128,2,3136]{2,1,0:T(2,128)(2,1)S(1)}, u32[]{:S(2)}, u32[]{:S(2)}) %all-to-all-start.2) | async-done | bytes 1605664 | tf_op jit(solution)/shard_map/all_to_all | solution.py:153
  643.2 10.7 %reshape.579 = bf16[896,1,7,2,4,16]{5,4,3,2,1,0:T(4,128)(2,1)} reshape(bf16[128,2,3136]{2,1,0:T(2,128)(2,1)S(1)} %all-to-all-done.2) | data formatting | bytes 3211264
  654.0 21.4 %copy.240 = bf16[1,7,2,4,16,128,7]{5,4,1,3,6,2,0:T(8,128)(2,1)S(1)} copy(bf16[1,7,2,4,16,128,7]{4,3,2,1,6,5,0:T(4,128)(2,1)} %bitcast.194) | data formatting | bytes 3211264 | tf_op jit(solution)/shard_map/all_to_all | solution.py:153
  675.3 232.5 %fusion.27 = bf16[7,2,16,3584]{3,2,0,1:T(8,128)(2,1)S(1)} fusion(f32[128,7,4]{0,1,2:T(8,128)S(1)} %compare_select_fusion, s32[128,7,4]{0,1,2:T(8,128)S(1)} %broadcast_select_fusion.3, pred[4]{0:T(512)(128)(4,1)S(1)} %copy-done.16, bf16[1,7,2,4,16,128,7]{5,4,1,3,6,2,0:T(8,128)(2,1)S(1)} %copy.240, f32[7,2,3584]{2,0,1:T(8,128)S(1)} %copy-done.6), kind=kOutput, calls=%fused_computation.37 | convolution fusion | flops 5936021504 | bytes 3440644 | tf_op jit(solution)/shard_map/swhapj,swal->jhpl/dot_general | solution.py:157
  907.8 1.3 copy.241
  (100 shorter events, 12.9 us)
Async XLA Ops:
  0.7 290.9 %all-to-all-start = ((bf16[128,7,1,1,1,1]{1,5,4,3,2,0:T(2,128)(2,1)}), bf16[128,7,1,1,1,1]{1,5,4,3,2,0:T(2,128)(2,1)S(1)}, u32[]{:S(2)}, u32[]{:S(2)}) async-start(bf16[128,7,1,1,1,1]{1,5,4,3,2,0:T(2,128)(2,1)} %broadcast_in_dim.185), calls=%async_computation | async-start | bytes 131072 | tf_op jit(solution)/shard_map/all_to_all | solution.py:133
  12.2 20.0 %copy-start.12 = (pred[4]{0:T(512)(128)(4,1)}, pred[4]{0:T(512)(128)(4,1)S(1)}, u32[]{:S(2)}) copy-start(pred[4]{0:T(512)(128)(4,1)S(1)} %iota_compare_fusion.2) | copy-start | bytes 16
  12.2 1.7 copy-start.15
  13.5 18.7 %copy-start.9 = (s32[896]{0:T(1024)}, s32[896]{0:T(1024)S(1)}, u32[]{:S(2)}) copy-start(s32[896]{0:T(1024)S(1)} %broadcast_subtract_fusion) | copy-start | bytes 10756
  14.9 17.3 %copy-start.5 = (f32[7,2,3584]{2,0,1:T(8,128)}, f32[7,2,3584]{2,0,1:T(8,128)S(1)}, u32[]{:S(2)}) copy-start(f32[7,2,3584]{2,0,1:T(8,128)S(1)} %copy.210) | copy-start | bytes 602116
  16.1 16.1 %copy-start.4 = (bf16[7,2,16,3584]{3,2,1,0:T(8,128)(2,1)S(1)}, bf16[7,2,16,3584]{3,2,1,0:T(8,128)(2,1)}, u32[]{:S(2)}) copy-start(bf16[7,2,16,3584]{3,2,1,0:T(8,128)(2,1)} %param.5) | copy-start | bytes 4816900
  291.5 160.8 %all-to-all-start.1 = ((bf16[128,2,3136]{2,1,0:T(2,128)(2,1)}), bf16[128,2,3136]{2,1,0:T(2,128)(2,1)S(1)}, u32[]{:S(2)}, u32[]{:S(2)}) async-start(bf16[128,2,3136]{2,1,0:T(2,128)(2,1)} %reshape.576), calls=%async_computation.1 | async-start | bytes 3276800 | tf_op jit(solution)/shard_map/all_to_all | solution.py:132
  409.7 23.4 %copy-start = (bf16[7,448,2,896]{3,2,1,0:T(2,128)(2,1)S(1)}, bf16[7,448,2,896]{3,2,1,0:T(2,128)(2,1)}, u32[]{:S(2)}) copy-start(bf16[7,448,2,896]{3,2,1,0:T(2,128)(2,1)} %reshape.520) | copy-start | bytes 33718276
  433.1 18.4 %copy-start.1 = (s32[896]{0:T(1024)S(1)}, s32[896]{0:T(1024)}, u32[]{:S(2)}) copy-start(s32[896]{0:T(1024)} %param.8) | copy-start | bytes 10756
  433.1 19.1 %copy-start.11 = (s32[1793]{0:T(1024)S(1)}, s32[1793]{0:T(1024)}, u32[]{:S(2)}) copy-start(s32[1793]{0:T(1024)} %iota_add_fusion) | copy-start | bytes 21520
  469.2 15.5 %copy-start.14 = (s32[896]{0:T(1024)S(1)}, s32[896]{0:T(1024)}, u32[]{:S(2)}) copy-start(s32[896]{0:T(1024)} %param.7) | copy-start | bytes 10756
  484.7 17.0 %slice-start.3 = ((s8[11239424]{0:T(1024)(128)(4,1)}), s8[4194304]{0:T(1024)(128)(4,1)S(1)}, s32[]{:S(2)}) async-start(s8[11239424]{0:T(1024)(128)(4,1)} %bitcast.200), calls=%async_computation.6 | async-start | bytes 8388608
  484.7 17.1 %slice-start.4 = ((s8[11239424]{0:T(1024)(128)(4,1)}), s8[4194304]{0:T(1024)(128)(4,1)S(1)}, s32[]{:S(2)}) async-start(s8[11239424]{0:T(1024)(128)(4,1)} %bitcast.200), calls=%async_computation.7 | async-start | bytes 8388608
  494.0 9.7 %copy-start.2 = (bf16[7,4,1,16,896]{4,3,2,1,0:T(8,128)(2,1)}, bf16[7,4,1,16,896]{4,3,2,1,0:T(8,128)(2,1)S(1)}, u32[]{:S(2)}) copy-start(bf16[7,4,1,16,896]{4,3,2,1,0:T(8,128)(2,1)S(1)} %get-tuple-element.22) | copy-start | bytes 2408452
  494.0 9.7 %copy-start.3 = (bf16[7,4,1,16,896]{4,3,2,1,0:T(8,128)(2,1)}, bf16[7,4,1,16,896]{4,3,2,1,0:T(8,128)(2,1)S(1)}, u32[]{:S(2)}) copy-start(bf16[7,4,1,16,896]{4,3,2,1,0:T(8,128)(2,1)S(1)} %get-tuple-element.21) | copy-start | bytes 2408452
  494.2 7.6 slice-start.5
  542.5 14.0 %copy-start.7 = (bf16[7,448,32]{1,2,0:T(8,128)(2,1)S(1)}, bf16[7,448,32]{1,2,0:T(8,128)(2,1)}, u32[]{:S(2)}) copy-start(bf16[7,448,32]{1,2,0:T(8,128)(2,1)} %get-tuple-element.31) | copy-start | bytes 602116
  545.5 10.9 %copy-start.8 = (bf16[7,448,32]{1,2,0:T(8,128)(2,1)S(1)}, bf16[7,448,32]{1,2,0:T(8,128)(2,1)}, u32[]{:S(2)}) copy-start(bf16[7,448,32]{1,2,0:T(8,128)(2,1)} %get-tuple-element.32) | copy-start | bytes 602116
  550.9 16.3 %slice-start = ((s8[11239424]{0:T(1024)(128)(4,1)}), s8[4194304]{0:T(1024)(128)(4,1)S(1)}, s32[]{:S(2)}) async-start(s8[11239424]{0:T(1024)(128)(4,1)} %bitcast.198), calls=%async_computation.3 | async-start | bytes 8388608
  550.9 16.3 %slice-start.1 = ((s8[11239424]{0:T(1024)(128)(4,1)}), s8[4194304]{0:T(1024)(128)(4,1)S(1)}, s32[]{:S(2)}) async-start(s8[11239424]{0:T(1024)(128)(4,1)} %bitcast.198), calls=%async_computation.4 | async-start | bytes 8388608
  556.5 10.7 %slice-start.2 = ((s8[11239424]{0:T(1024)(128)(4,1)}), s8[2850816]{0:T(1024)(128)(4,1)S(1)}, s32[]{:S(2)}) async-start(s8[11239424]{0:T(1024)(128)(4,1)} %bitcast.198), calls=%async_computation.5 | async-start | bytes 5701632
  589.7 28.8 %copy-start.10 = (s32[896]{0:T(1024)S(1)}, s32[896]{0:T(1024)}, u32[]{:S(2)}) copy-start(s32[896]{0:T(1024)} %copy-done.9) | copy-start | bytes 10756
  589.7 29.3 %copy-start.13 = (pred[4]{0:T(512)(128)(4,1)S(1)}, pred[4]{0:T(512)(128)(4,1)}, u32[]{:S(2)}) copy-start(pred[4]{0:T(512)(128)(4,1)} %copy-done.12) | copy-start | bytes 16
  608.4 34.8 %all-to-all-start.2 = ((bf16[128,2,3136]{2,1,0:T(2,128)(2,1)}), bf16[128,2,3136]{2,1,0:T(2,128)(2,1)S(1)}, u32[]{:S(2)}, u32[]{:S(2)}) async-start(bf16[128,2,3136]{2,1,0:T(2,128)(2,1)} %reshape.578), calls=%async_computation.2 | async-start | bytes 3276800 | tf_op jit(solution)/shard_map/all_to_all | solution.py:153
  619.2 56.1 %copy-start.6 = (f32[7,2,3584]{2,0,1:T(8,128)S(1)}, f32[7,2,3584]{2,0,1:T(8,128)}, u32[]{:S(2)}) copy-start(f32[7,2,3584]{2,0,1:T(8,128)} %copy-done.5) | copy-start | bytes 602116
  619.2 56.1 %copy-start.16 = (pred[4]{0:T(512)(128)(4,1)S(1)}, pred[4]{0:T(512)(128)(4,1)}, u32[]{:S(2)}) copy-start(pred[4]{0:T(512)(128)(4,1)} %copy-done.15) | copy-start | bytes 16
where the time goes:
time: 915 us; the launch traced here: 909 us
  matrix products  503 us (55%)
  local copies, waits for them, and re-layouts  311 us (34%)
  other arithmetic  38.6 us (4%)
  starting transfers between devices  31.4 us (3%)
  waiting for transfers between devices  24 us (3%)
    dot_general x1, matrix products, per_device(): jnp.einsum('swhapj,swal->jhpl', spectral, backward, preferred_element_typ...  232 us
    dot_general x1, matrix products, per_device(): jnp.einsum('lc,jhpl->chpj', forward_table(pair_order, degrees, longitudes...  221 us
    unnamed x57, local copies, waits for them, and re-layouts  70.2 us
    gather x6, local copies, waits for them, and re-layouts, per_device(): slot_tables = jnp.take(legendre_table, slot_ids, axis=0)  38.3 us
    select_n x1, other arithmetic, per_device(): slot_tables = jnp.take(legendre_table, slot_ids, axis=0)  25.7 us
    all_to_all x1, waiting for transfers between devices, per_device(): lax.all_to_all(answer[None], ('grp', 'dev'), split_axis=5, concat_axis=0,...  24 us
    slice x1, local copies, waits for them, and re-layouts, legendre(): lower_prod = across_lat(lower[:, side], joined)  23.4 us
    reshape x1, local copies, waits for them, and re-layouts, legendre(): lower = table_rows[half:degrees].reshape(half // 2, 2, circle_half)  22.6 us
  transfers between devices with their start and end apart: 3, of which 1 were waited for; matrix products, arithmetic and copies ran while one was open for 47% of the time, Pallas kernels for 0%

commit v1 on v0

v1 whole, which is shorter than its diff:
```python
import functools
import math

import jax
import jax.numpy as jnp
import numpy as np
from jax import lax
from jax.experimental import pallas as pl
from jax.experimental.pallas import tpu as pltpu
from jax.sharding import PartitionSpec as P

AXES = ("grp", "dev")
RADIX = 14
HALF = RADIX // 2
BLOCK = 256
WAVES = 128
NN = (((1,), (0,)), ((), ()))
NT = (((1,), (1,)), ((), ()))
TN = (((0,), (0,)), ((), ()))


def dot(left, right, dims=NN):
    return lax.dot_general(left, right, dims, preferred_element_type=jnp.float32)


@functools.lru_cache(None)
def fourier_tables(longitudes):
    degrees = longitudes // 2
    place = np.arange(BLOCK)
    wave = np.arange(WAVES)
    ahead = np.zeros((2, HALF, 2 * BLOCK, 2 * WAVES), np.float64)
    back = np.zeros((2, HALF, 2 * WAVES, 2 * BLOCK), np.float64)
    for side in range(2):
        for c in range(HALF):
            m = RADIX * wave + c
            if side:
                m = degrees - 1 - m
            angle = 2.0 * np.pi * ((m[None, :] * place[:, None]) % longitudes) / longitudes
            cos, sin = np.cos(angle), np.sin(angle)
            sign = -1.0 if side else 1.0
            ahead[side, c] = np.block([[cos, -sin], [sign * sin, sign * cos]]) * longitudes ** -0.5
            weight = np.where(m == 0, 1.0, 2.0)[:, None] * longitudes ** -0.5
            back[side, c] = np.block(
                [
                    [weight * cos.T, sign * weight * sin.T],
                    [-weight * sin.T, sign * weight * cos.T],
                ]
            )
    kind = jnp.bfloat16
    return ahead.astype(np.float32).astype(kind), back.astype(np.float32).astype(kind)


def ring(turns):
    angle = 2.0 * math.pi * (turns % RADIX) / RADIX
    return math.cos(angle), math.sin(angle)


def analyse_kernel(probe_ref, kappa_ref, table_ref, rep_ref, out_ref, y_ref, four_ref, wide_ref):
    rows = probe_ref.shape[1]
    circles = kappa_ref.shape[0]
    groups = 2 * circles

    def fold(circle, side):
        group = 2 * circle + side
        at = pl.ds(pl.multiple_of(group * rows, rows), rows)
        for lane in range(0, BLOCK, 128):
            x = []
            for b in range(RADIX):
                cut = pl.ds(b * BLOCK + lane, 128)
                scale = kappa_ref[circle, side : side + 1, cut]
                x.append(
                    (probe_ref[group, :, cut].astype(jnp.float32) * scale)
                    .astype(jnp.bfloat16)
                    .astype(jnp.float32)
                )
            s = [x[b] + x[b + HALF] for b in range(HALF)]
            d = [x[b] - x[b + HALF] for b in range(HALF)]
            even_re = [s[b] + s[HALF - b] for b in range(1, 4)]
            even_im = [s[b] - s[HALF - b] for b in range(1, 4)]
            odd_re = [d[b] - d[HALF - b] for b in range(1, 4)]
            odd_im = [d[b] + d[HALF - b] for b in range(1, 4)]
            for j in range(HALF + 1):
                first, re_terms, im_terms = (
                    (s[0], even_re, even_im) if j % 2 == 0 else (d[0], odd_re, odd_im)
                )
                real = first
                for b in range(1, 4):
                    real = real + re_terms[b - 1] * ring(j * b)[0]
                y_ref[j, at, pl.ds(lane, 128)] = real.astype(jnp.bfloat16)
                if 0 < j < HALF:
                    imag = -(im_terms[0] * ring(j)[1])
                    for b in range(2, 4):
                        imag = imag - im_terms[b - 1] * ring(j * b)[1]
                    y_ref[j, at, pl.ds(BLOCK + lane, 128)] = imag.astype(jnp.bfloat16)

    def fold_circle(circle, carry):
        fold(circle, 0)
        fold(circle, 1)
        return carry

    lax.fori_loop(0, circles, fold_circle, 0)
    for side in range(2):
        for c in range(HALF):
            j = c + side
            depth = BLOCK if j in (0, HALF) else 2 * BLOCK
            coef = dot(y_ref[j, :, :depth], table_ref[side, c, :depth, :]).astype(jnp.bfloat16)
            for group in range(groups):
                for part in range(2):
                    base = group * 4 * rows + (2 * side + part) * rows
                    four_ref[base : base + rows, c * WAVES : (c + 1) * WAVES] = coef[
                        group * rows : (group + 1) * rows, part * WAVES : (part + 1) * WAVES
                    ]
    reps = four_ref.shape[1]
    width = 8 * rows
    devices = rep_ref.shape[0] // circles
    for item in range(7):
        wide_ref[item, pl.ds(7, devices, stride=8), :] = jnp.zeros((devices, width), jnp.float32)
    lanes = lax.broadcasted_iota(jnp.int32, (devices, reps), 1)
    four = four_ref[...]
    for item in range(7):
        pick = jnp.where((rep_ref[item * devices : (item + 1) * devices, :] == lanes), 1.0, 0.0).astype(jnp.bfloat16)
        moved = dot(pick, four, NT)
        for t in range(circles):
            wide_ref[item, pl.ds(t, devices, stride=8), :] = moved[:, t * width : (t + 1) * width]
        out_ref[:, item * width : (item + 1) * width] = wide_ref[item].astype(jnp.bfloat16)


def legendre_kernel(
    pair_ref, coming_ref, table_ref, row_ref, col_ref, out_ref, x_ref, b_ref, wide_ref
):
    item = pl.program_id(0)
    items = pl.num_programs(0)
    circle_half = x_ref.shape[2]
    width = x_ref.shape[1]
    degrees = table_ref.shape[1] - 1
    half_width = width // 2

    @pl.when(item == 0)
    def _():
        slots = coming_ref.shape[0]
        where = lax.broadcasted_iota(jnp.int32, (circle_half, slots), 0)
        pick = jnp.where((row_ref[...] == where), 1.0, 0.0).astype(jnp.bfloat16)
        natural = dot(pick, coming_ref[...])
        low = lax.broadcasted_iota(jnp.int32, (circle_half, width), 1) < half_width
        for i in range(x_ref.shape[0]):
            x = natural[:, i * width : (i + 1) * width]
            other = pltpu.roll(x, half_width, 1)
            x_ref[i] = jnp.where(low, x + other, other - x).T.astype(jnp.bfloat16)

    q = pair_ref[item]
    swap = (q % RADIX >= HALF).astype(jnp.int32)

    def weights(first, count):
        row = lax.broadcasted_iota(jnp.int32, (1, count), 1) + first
        second = row >= degrees - q
        degree = jnp.where(second, row - 1, q + row).astype(jnp.float32)
        damping = 1.0 / (1.0 + 4.0 * degree * (degree + 1.0) / float(degrees * degrees))
        wave = second.astype(jnp.int32) ^ swap
        parity = jnp.where(second, row + q, row) & 1
        code = 2 * parity + wave
        return [jnp.where(code == k, damping, 0.0) for k in range(4)]

    quarter = width // 4
    spectrum = dot(x_ref[item], table_ref[0, :degrees, :], NT)
    last_row = table_ref[0, degrees:, :].astype(jnp.float32)
    last = jnp.sum(x_ref[item].astype(jnp.float32) * last_row, axis=1, keepdims=True)
    main_weights = weights(0, degrees)
    last_weights = weights(degrees, 1)
    scaled = jnp.concatenate(
        [
            (spectrum[k * quarter : (k + 1) * quarter] * main_weights[k]).astype(jnp.bfloat16)
            for k in range(4)
        ],
        axis=0,
    )
    scaled_last = jnp.concatenate(
        [
            (last[k * quarter : (k + 1) * quarter] * last_weights[k])
            .astype(jnp.bfloat16)
            .astype(jnp.float32)
            for k in range(4)
        ],
        axis=0,
    )
    total = dot(scaled, table_ref[0, :degrees, :])
    total = total + scaled_last * last_row
    even, odd = total[:half_width], total[half_width:]
    base = pl.multiple_of(item * width, width)
    b_ref[pl.ds(base, half_width), :] = (even + odd).astype(jnp.bfloat16)
    b_ref[pl.ds(base + half_width, half_width), :] = (even - odd).astype(jnp.bfloat16)

    @pl.when(item == items - 1)
    def _():
        devices = wide_ref.shape[1] // 8
        circles = col_ref.shape[0] // devices
        for t in range(circles):
            wide_ref[t, pl.ds(7, devices, stride=8), :] = jnp.zeros((devices, width), jnp.float32)
        lanes = lax.broadcasted_iota(jnp.int32, (devices, circle_half), 1)
        back = b_ref[...]
        for t in range(circles):
            pick = jnp.where((col_ref[t * devices : (t + 1) * devices, :] == lanes), 1.0, 0.0).astype(jnp.bfloat16)
            moved = dot(pick, back, NT)
            for i in range(7):
                wide_ref[t, pl.ds(i, devices, stride=8), :] = moved[:, i * width : (i + 1) * width]
            out_ref[:, t * width : (t + 1) * width] = wide_ref[t].astype(jnp.bfloat16)


def synthesise_kernel(coming_ref, kappa_ref, table_ref, rep_ref, out_ref, left_ref, u_ref):
    rows = out_ref.shape[1]
    circles = kappa_ref.shape[0]
    groups = 2 * circles
    width = 8 * rows
    slots = coming_ref.shape[0]
    reps = HALF * WAVES
    lanes = lax.broadcasted_iota(jnp.int32, (slots, reps), 1)
    pick = jnp.where((rep_ref[...] == lanes), 1.0, 0.0).astype(jnp.bfloat16)
    for t in range(circles):
        coef = dot(coming_ref[:, t * width : (t + 1) * width], pick, TN).astype(jnp.bfloat16)
        for side in range(2):
            group = 2 * t + side
            for part in range(4):
                base = side * 4 * rows + part * rows
                for c in range(HALF):
                    left_ref[
                        c + part // 2,
                        group * rows : (group + 1) * rows,
                        part * WAVES : (part + 1) * WAVES,
                    ] = coef[base : base + rows, c * WAVES : (c + 1) * WAVES]
    two = 2 * WAVES
    for j in range(HALF + 1):
        if j == 0:
            u_ref[j, :, :BLOCK] = dot(left_ref[j, :, :two], table_ref[0, 0, :, :BLOCK])
        elif j == HALF:
            u_ref[j, :, :BLOCK] = dot(left_ref[j, :, two:], table_ref[1, j - 1, :, :BLOCK])
        else:
            u_ref[j] = dot(left_ref[j, :, :two], table_ref[0, j]) + dot(
                left_ref[j, :, two:], table_ref[1, j - 1]
            )

    def unfold(circle, side):
        group = 2 * circle + side
        at = pl.ds(pl.multiple_of(group * rows, rows), rows)
        for lane in range(0, BLOCK, 128):
            real = [u_ref[j, at, pl.ds(lane, 128)] for j in range(HALF + 1)]
            imag = [None] + [u_ref[j, at, pl.ds(BLOCK + lane, 128)] for j in range(1, HALF)]
            value = [None] * RADIX
            for b in range(4):
                cos_even = real[0]
                for j in (2, 4, 6):
                    cos_even = cos_even + real[j] * ring(j * b)[0]
                cos_odd = real[HALF] * ring(HALF * b)[0]
                for j in (1, 3, 5):
                    cos_odd = cos_odd + real[j] * ring(j * b)[0]
                if b == 0:
                    value[0] = cos_even + cos_odd
                    value[HALF] = cos_even - cos_odd
                    continue
                sin_even = imag[2] * ring(2 * b)[1]
                for j in (4, 6):
                    sin_even = sin_even + imag[j] * ring(j * b)[1]
                sin_odd = imag[1] * ring(b)[1]
                for j in (3, 5):
                    sin_odd = sin_odd + imag[j] * ring(j * b)[1]
                up, down = cos_even + cos_odd, cos_even - cos_odd
                sup, sdown = sin_even + sin_odd, sin_even - sin_odd
                value[b] = up - sup
                value[RADIX - b] = up + sup
                value[HALF + b] = down - sdown
                value[HALF - b] = down + sdown
            for b in range(RADIX):
                cut = pl.ds(b * BLOCK + lane, 128)
                scale = kappa_ref[circle, side : side + 1, cut]
                out_ref[group, :, cut] = (value[b] * scale).astype(jnp.bfloat16)

    def unfold_circle(circle, carry):
        unfold(circle, 0)
        unfold(circle, 1)
        return carry

    lax.fori_loop(0, circles, unfold_circle, 0)


LIMIT = pltpu.CompilerParams(vmem_limit_bytes=56 * 2**20)
VMEM = pl.BlockSpec(memory_space=pltpu.VMEM)


def per_device(probe_field, kappa_field, circle_order, pair_order, legendre_table):
    circles, sides, probes, longitudes = probe_field.shape
    items, row_count, circle_half = legendre_table.shape
    devices = lax.axis_size(AXES)
    groups = circles * sides
    reps = HALF * WAVES
    width = 8 * probes
    ahead, back = fourier_tables(longitudes)
    ahead, back = jnp.asarray(ahead), jnp.asarray(back)

    kind, step = pair_order % RADIX, pair_order // RADIX
    rep = jnp.where(
        kind < HALF, kind * WAVES + step, (RADIX - 1 - kind) * WAVES + (WAVES - 1 - step)
    ).reshape(devices, items)
    rep_by_item = rep.T.reshape(-1, 1)
    rep_by_device = jnp.pad(rep, ((0, 0), (0, 8 - items)), constant_values=-1).reshape(-1, 1)
    circle = circle_order.reshape(devices, circles)
    circle_row = jnp.pad(circle, ((0, 0), (0, 8 - circles)), constant_values=-1).reshape(1, -1)
    circle_col = circle.T.reshape(-1, 1)
    pairs = lax.dynamic_slice(pair_order, (lax.axis_index(AXES) * items,), (items,))

    bf16, f32 = jnp.bfloat16, jnp.float32
    sending = pl.pallas_call(
        analyse_kernel,
        out_shape=jax.ShapeDtypeStruct((devices * 8, items * width), bf16),
        in_specs=[VMEM] * 4,
        out_specs=VMEM,
        scratch_shapes=[
            pltpu.VMEM((HALF + 1, groups * probes, 2 * BLOCK), bf16),
            pltpu.VMEM((circles * width, reps), bf16),
            pltpu.VMEM((items, devices * 8, width), f32),
        ],
        compiler_params=LIMIT,
        name="analyse",
    )(probe_field.reshape(groups, probes, longitudes), kappa_field, ahead, rep_by_item)

    coming = lax.all_to_all(
        sending.reshape(devices, 8, items * width), AXES, split_axis=0, concat_axis=0, tiled=True
    ).reshape(devices * 8, items * width)

    sending = pl.pallas_call(
        legendre_kernel,
        out_shape=jax.ShapeDtypeStruct((devices * 8, circles * width), bf16),
        grid_spec=pltpu.PrefetchScalarGridSpec(
            num_scalar_prefetch=1,
            grid=(items,),
            in_specs=[
                VMEM,
                pl.BlockSpec((1, row_count, circle_half), lambda i, s: (i, 0, 0)),
                VMEM,
                VMEM,
            ],
            out_specs=VMEM,
            scratch_shapes=[
                pltpu.VMEM((items, width, circle_half), bf16),
                pltpu.VMEM((items * width, circle_half), bf16),
                pltpu.VMEM((circles, devices * 8, width), f32),
            ],
        ),
        compiler_params=LIMIT,
        name="legendre",
    )(pairs, coming, legendre_table, circle_row, circle_col)

    coming = lax.all_to_all(
        sending.reshape(devices, 8, circles * width), AXES, split_axis=0, concat_axis=0, tiled=True
    ).reshape(devices * 8, circles * width)

    filtered = pl.pallas_call(
        synthesise_kernel,
        out_shape=jax.ShapeDtypeStruct((groups, probes, longitudes), bf16),
        in_specs=[VMEM] * 4,
        out_specs=VMEM,
        scratch_shapes=[
            pltpu.VMEM((HALF + 1, groups * probes, 4 * WAVES), bf16),
            pltpu.VMEM((HALF + 1, groups * probes, 2 * BLOCK), f32),
        ],
        compiler_params=LIMIT,
        name="synthesise",
    )(coming, kappa_field, back, rep_by_device)
    return filtered.reshape(circles, sides, probes, longitudes)


def solution(mesh):
    return jax.shard_map(
        per_device,
        mesh=mesh,
        in_specs=(
            P(AXES, None, None, None),
            P(AXES, None, None),
            P(),
            P(),
            P(AXES, None, None),
        ),
        out_specs=P(AXES, None, None, None),
        check_vma=False,
    )
```

time: 915 us -> 116 us (0.13)
  matrix products: 503 us -> 0 us
  local copies, waits for them, and re-layouts: 311 us -> 8.08 us
  Pallas kernels: 0 us -> 41.2 us
  other arithmetic: 38.6 us -> 0.7 us
  waiting for transfers between devices: 24 us -> 49.7 us
  starting transfers between devices: 31.4 us -> 16.1 us
    dot_general x13 -> x0, matrix products: 503 us -> none  [the longest x1 232 us: per_device(): jnp.einsum('swhapj,swal->jhpl', spectral, backward, preferred_element_typ...]
    unnamed x57 -> x10, local copies, waits for them, and re-layouts: 70.2 us -> 4.53 us
    slice x7 -> x0, local copies, waits for them, and re-layouts: 64.1 us -> none  [the longest x1 23.4 us: legendre(): lower_prod = across_lat(lower[:, side], joined)]
    reshape x3 -> x4, local copies, waits for them, and re-layouts: 55 us -> 2.09 us  [the longest x1 1 us: per_device(): jnp.pad(rep, ((0, 0), (0, 8 - items)), constant_values=-1).reshape(-1, 1)]
    all_to_all x4 -> x0, local copies, waits for them, and re-layouts: 43.1 us -> none  [the longest x2 21.7 us: per_device(): lax.all_to_all(payload, ('grp', 'dev'), split_axis=0, concat_axis=5, tile...]
    pallas_call x0 -> x3, Pallas kernels: none -> 41.2 us  [the longest x1 23.4 us: per_device(): pl.pallas_call(legendre_kernel, out_shape=jax.ShapeDtypeStruct((devices *...]
    gather x7 -> x0, local copies, waits for them, and re-layouts: 38.9 us -> none  [the longest x6 38.3 us: per_device(): slot_tables = jnp.take(legendre_table, slot_ids, axis=0)]
    select_n x8 -> x1, other arithmetic: 28.7 us -> 0.7 us  [per_device(): jnp.where(kind < HALF, kind * WAVES + step, (RADIX - 1 - kind) * WAVES +...]
  transfers between devices with their start and end apart: 3 -> 2, of which waited for: 1 -> 2; matrix products, arithmetic and copies ran while one was open for 47% -> 4% of each run, Pallas kernels for 0% -> 0%
where the time goes in v1:
time: 116 us
  waiting for transfers between devices  49.7 us (43%)
  Pallas kernels  41.2 us (36%)
  starting transfers between devices  16.1 us (14%)
  local copies, waits for them, and re-layouts  8.08 us (7%)
    all_to_all x1, waiting for transfers between devices, per_device(): lax.all_to_all(sending.reshape(devices, 8, circles * width), AXES, split_...  26.1 us
    all_to_all x1, waiting for transfers between devices, per_device(): lax.all_to_all(sending.reshape(devices, 8, items * width), AXES, split_ax...  23.6 us
    pallas_call x1, Pallas kernels, per_device(): pl.pallas_call(legendre_kernel, out_shape=jax.ShapeDtypeStruct((devices *...  23.4 us
    all_to_all x1, starting transfers between devices, per_device(): lax.all_to_all(sending.reshape(devices, 8, items * width), AXES, split_ax...  11.5 us
    pallas_call x1, Pallas kernels, per_device(): pl.pallas_call(analyse_kernel, out_shape=jax.ShapeDtypeStruct((devices *...  9.69 us
    pallas_call x1, Pallas kernels, per_device(): pl.pallas_call(synthesise_kernel, out_shape=jax.ShapeDtypeStruct((groups,...  8.07 us
    all_to_all x1, starting transfers between devices, per_device(): lax.all_to_all(sending.reshape(devices, 8, circles * width), AXES, split_...  4.64 us
    unnamed x10, local copies, waits for them, and re-layouts  4.53 us
  transfers between devices with their start and end apart: 2, of which 2 were waited for; matrix products, arithmetic and copies ran while one was open for 4% of the time, Pallas kernels for 0%

profile of v1, /device:TPU:1, one launch (start us, length us, event | category | flops | bytes accessed | tf_op | source)
XLA Modules:
  0.0 115.8 jit_solution(2772624777612842174)
XLA Ops:
  0.0 0.7 add_select_fusion.2
  0.7 0.2 reshape.37
  0.9 0.1 copy.10
  1.0 1.0 copy.16
  2.0 9.7 %analyse.1 = bf16[1024,896]{1,0:T(8,128)(2,1)} custom-call(bf16[14,16,3584]{2,1,0:T(8,128)(2,1)} %bitcast.26, f32[7,2,3584]{2,1,0:T(2,128)} %kappa_ref.3, bf16[2,7,512,256]{3,2,1,0:T(8,128)(2,1)} %constant.48.clone.table_ref, s32[896,1]{1,0:T(8,128)} %bitcast.24), custom_call_target="tpu_custom_call" | custom-call | tf_op jit(solution)/shard_map/analyse/pallas_call | solution.py:309
  11.7 0.0 copy-start.2
  11.7 11.5 %all-to-all-start = ((bf16[128,8,896]{2,1,0:T(8,128)(2,1)}), bf16[128,8,896]{2,1,0:T(8,128)(2,1)S(1)}, u32[]{:S(2)}, u32[]{:S(2)}) async-start(bf16[128,8,896]{2,1,0:T(8,128)(2,1)} %bitcast.20), calls=%async_computation | async-start | bytes 3670016 | tf_op jit(solution)/shard_map/all_to_all | solution.py:323
  23.2 1.3 %dynamic_slice.3.pair_ref = s32[7]{0:T(128)} dynamic-slice(s32[896]{0:T(1024)} %param.10, s32[]{:T(128)S(6)} %select_n.18), dynamic_slice_sizes={7} | dynamic-slice | bytes 60 | tf_op jit(solution)/shard_map/dynamic_slice | solution.py:306
  24.5 0.0 copy-done.2
  24.5 0.2 reshape.41
  24.7 0.1 copy.12
  24.8 1.0 copy.18
  25.8 0.7 reshape.42.row_ref
  26.5 23.6 %all-to-all-done = bf16[128,8,896]{2,1,0:T(8,128)(2,1)S(1)} async-done(((bf16[128,8,896]{2,1,0:T(8,128)(2,1)}), bf16[128,8,896]{2,1,0:T(8,128)(2,1)S(1)}, u32[]{:S(2)}, u32[]{:S(2)}) %all-to-all-start) | async-done | bytes 1835040 | tf_op jit(solution)/shard_map/all_to_all | solution.py:323
  50.1 0.0 copy-start.1
  50.1 1.2 %copy-done.1 = bf16[128,8,896]{2,1,0:T(8,128)(2,1)} copy-done((bf16[128,8,896]{2,1,0:T(8,128)(2,1)}, bf16[128,8,896]{2,1,0:T(8,128)(2,1)S(1)}, u32[]{:S(2)}) %copy-start.1) | copy-done | bytes 1835032
  51.4 23.4 %legendre.1 = bf16[1024,896]{1,0:T(8,128)(2,1)} custom-call(s32[7]{0:T(128)} %dynamic_slice.3.pair_ref, bf16[1024,896]{1,0:T(8,128)(2,1)} %bitcast.22, bf16[7,1793,896]{2,1,0:T(8,128)(2,1)} %table_ref.3, s32[1,1024]{1,0:T(1,128)} %reshape.42.row_ref, s32[896,1]{1,0:T(8,128)} %bitcast.25), custom_call_target="tpu_custom_call" | custom-call | tf_op jit(solution)/shard_map/legendre/pallas_call | solution.py:327
  74.8 4.6 %all-to-all-start.1 = ((bf16[128,8,896]{2,1,0:T(8,128)(2,1)}), bf16[128,8,896]{2,1,0:T(8,128)(2,1)S(1)}, u32[]{:S(2)}, u32[]{:S(2)}) async-start(bf16[128,8,896]{2,1,0:T(8,128)(2,1)} %bitcast.23), calls=%async_computation.1 | async-start | bytes 3670016 | tf_op jit(solution)/shard_map/all_to_all | solution.py:350
  79.5 1.0 reshape.50.rep_ref
  80.5 26.1 %all-to-all-done.1 = bf16[128,8,896]{2,1,0:T(8,128)(2,1)S(1)} async-done(((bf16[128,8,896]{2,1,0:T(8,128)(2,1)}), bf16[128,8,896]{2,1,0:T(8,128)(2,1)S(1)}, u32[]{:S(2)}, u32[]{:S(2)}) %all-to-all-start.1) | async-done | bytes 1835040 | tf_op jit(solution)/shard_map/all_to_all | solution.py:350
  106.5 0.0 copy-start
  106.5 1.2 %copy-done = bf16[128,8,896]{2,1,0:T(8,128)(2,1)} copy-done((bf16[128,8,896]{2,1,0:T(8,128)(2,1)}, bf16[128,8,896]{2,1,0:T(8,128)(2,1)S(1)}, u32[]{:S(2)}) %copy-start) | copy-done | bytes 1835032
  107.8 8.1 %synthesise.1 = bf16[14,16,3584]{2,1,0:T(8,128)(2,1)} custom-call(bf16[1024,896]{1,0:T(8,128)(2,1)} %bitcast.21, f32[7,2,3584]{2,1,0:T(2,128)} %kappa_ref.3, bf16[2,7,256,512]{3,2,1,0:T(8,128)(2,1)} %constant.49.clone.table_ref, s32[1024,1]{1,0:T(8,128)} %reshape.50.rep_ref), custom_call_target="tpu_custom_call" | custom-call | tf_op jit(solution)/shard_map/synthesise/pallas_call | solution.py:354
  (4 shorter events, 0.0 us)
Async XLA Ops:
  11.7 12.8 %copy-start.2 = (s32[896]{0:T(1024)S(1)}, s32[896]{0:T(1024)}, u32[]{:S(2)}) copy-start(s32[896]{0:T(1024)} %param.9) | copy-start | bytes 10756
  11.7 38.5 %all-to-all-start = ((bf16[128,8,896]{2,1,0:T(8,128)(2,1)}), bf16[128,8,896]{2,1,0:T(8,128)(2,1)S(1)}, u32[]{:S(2)}, u32[]{:S(2)}) async-start(bf16[128,8,896]{2,1,0:T(8,128)(2,1)} %bitcast.20), calls=%async_computation | async-start | bytes 3670016 | tf_op jit(solution)/shard_map/all_to_all | solution.py:323
  50.1 1.2 %copy-start.1 = (bf16[128,8,896]{2,1,0:T(8,128)(2,1)}, bf16[128,8,896]{2,1,0:T(8,128)(2,1)S(1)}, u32[]{:S(2)}) copy-start(bf16[128,8,896]{2,1,0:T(8,128)(2,1)S(1)} %all-to-all-done) | copy-start | bytes 5505028
  74.8 31.7 %all-to-all-start.1 = ((bf16[128,8,896]{2,1,0:T(8,128)(2,1)}), bf16[128,8,896]{2,1,0:T(8,128)(2,1)S(1)}, u32[]{:S(2)}, u32[]{:S(2)}) async-start(bf16[128,8,896]{2,1,0:T(8,128)(2,1)} %bitcast.23), calls=%async_computation.1 | async-start | bytes 3670016 | tf_op jit(solution)/shard_map/all_to_all | solution.py:350
  106.5 1.2 %copy-start = (bf16[128,8,896]{2,1,0:T(8,128)(2,1)}, bf16[128,8,896]{2,1,0:T(8,128)(2,1)S(1)}, u32[]{:S(2)}) copy-start(bf16[128,8,896]{2,1,0:T(8,128)(2,1)S(1)} %all-to-all-done.1) | copy-start | bytes 5505028

commit v2 on v1

v2 whole, which is shorter than its diff:
```python
import functools
import math

import jax
import jax.numpy as jnp
import numpy as np
from jax import lax
from jax.experimental import pallas as pl
from jax.experimental.pallas import tpu as pltpu
from jax.sharding import PartitionSpec as P

AXES = ("grp", "dev")
RADIX = 14
HALF = RADIX // 2
BLOCK = 256
WAVES = 128
NN = (((1,), (0,)), ((), ()))
NT = (((1,), (1,)), ((), ()))
TN = (((0,), (0,)), ((), ()))


def dot(left, right, dims=NN):
    return lax.dot_general(left, right, dims, preferred_element_type=jnp.float32)


@functools.lru_cache(None)
def fourier_tables(longitudes):
    degrees = longitudes // 2
    place = np.arange(BLOCK)
    wave = np.arange(WAVES)
    ahead = np.zeros((2, HALF, 2 * BLOCK, 2 * WAVES), np.float64)
    back = np.zeros((2, HALF, 2 * WAVES, 2 * BLOCK), np.float64)
    for side in range(2):
        for c in range(HALF):
            m = RADIX * wave + c
            if side:
                m = degrees - 1 - m
            angle = 2.0 * np.pi * ((m[None, :] * place[:, None]) % longitudes) / longitudes
            cos, sin = np.cos(angle), np.sin(angle)
            sign = -1.0 if side else 1.0
            ahead[side, c] = np.block([[cos, -sin], [sign * sin, sign * cos]]) * longitudes ** -0.5
            weight = np.where(m == 0, 1.0, 2.0)[:, None] * longitudes ** -0.5
            back[side, c] = np.block(
                [
                    [weight * cos.T, sign * weight * sin.T],
                    [-weight * sin.T, sign * weight * cos.T],
                ]
            )
    kind = jnp.bfloat16
    return ahead.astype(np.float32).astype(kind), back.astype(np.float32).astype(kind)


def ring(turns):
    angle = 2.0 * math.pi * (turns % RADIX) / RADIX
    return math.cos(angle), math.sin(angle)


def representative(pairs):
    step = jnp.floor((pairs + 0.5) * (1.0 / RADIX))
    kind = pairs - RADIX * step
    other = (RADIX - 1 - kind) * WAVES + (WAVES - 1 - step)
    return jnp.where(kind < HALF, kind * WAVES + step, other)


def column(row):
    return jnp.broadcast_to(row, (row.shape[1], row.shape[1])).T


def mark_rows(pick_ref, row):
    count = pick_ref.shape[1]
    lanes = lax.broadcasted_iota(jnp.int32, (128, 128), 1).astype(jnp.float32)
    for first in range(0, row.shape[1], 128):
        upright = column(row[:, first : first + 128])
        for start in range(0, count, 128):
            hit = jnp.where(upright == lanes + float(start), 1.0, 0.0)
            pick_ref[first : first + 128, start : start + 128] = hit.astype(jnp.bfloat16)


def analyse_kernel(
    probe_hbm,
    kappa_hbm,
    table_hbm,
    pair_ref,
    out_hbm,
    probe_ref,
    kappa_ref,
    table_ref,
    y_ref,
    four_ref,
    pick_ref,
    wide_ref,
    send_ref,
    probe_sem,
    kappa_sem,
    table_sem,
    out_sem,
):
    rows = probe_ref.shape[1]
    circles = kappa_ref.shape[0]
    groups = 2 * circles
    reps = four_ref.shape[1]
    width = 8 * rows
    devices = wide_ref.shape[1] // 8

    def probe_copy(circle):
        at = pl.ds(2 * circle, 2)
        return pltpu.make_async_copy(probe_hbm.at[at], probe_ref.at[at], probe_sem.at[circle])

    kappa_copy = pltpu.make_async_copy(kappa_hbm, kappa_ref, kappa_sem)
    kappa_copy.start()
    for t in range(circles):
        probe_copy(t).start()
    table_copy = pltpu.make_async_copy(table_hbm, table_ref, table_sem)
    mark_rows(pick_ref, representative(pair_ref[...].astype(jnp.float32)))
    for t in range(circles):
        wide_ref[t, pl.ds(7, devices, stride=8), :] = jnp.zeros((devices, width), jnp.float32)
    kappa_copy.wait()

    def fold(circle, side):
        group = 2 * circle + side
        at = pl.ds(pl.multiple_of(group * rows, rows), rows)
        for lane in range(0, BLOCK, 128):
            x = []
            for b in range(RADIX):
                cut = pl.ds(b * BLOCK + lane, 128)
                scale = kappa_ref[circle, side : side + 1, cut]
                x.append(
                    (probe_ref[group, :, cut].astype(jnp.float32) * scale)
                    .astype(jnp.bfloat16)
                    .astype(jnp.float32)
                )
            s = [x[b] + x[b + HALF] for b in range(HALF)]
            d = [x[b] - x[b + HALF] for b in range(HALF)]
            even_re = [s[b] + s[HALF - b] for b in range(1, 4)]
            even_im = [s[b] - s[HALF - b] for b in range(1, 4)]
            odd_re = [d[b] - d[HALF - b] for b in range(1, 4)]
            odd_im = [d[b] + d[HALF - b] for b in range(1, 4)]
            for j in range(HALF + 1):
                first, re_terms, im_terms = (
                    (s[0], even_re, even_im) if j % 2 == 0 else (d[0], odd_re, odd_im)
                )
                real = first
                for b in range(1, 4):
                    real = real + re_terms[b - 1] * ring(j * b)[0]
                y_ref[j, at, pl.ds(lane, 128)] = real.astype(jnp.bfloat16)
                if 0 < j < HALF:
                    imag = -(im_terms[0] * ring(j)[1])
                    for b in range(2, 4):
                        imag = imag - im_terms[b - 1] * ring(j * b)[1]
                    y_ref[j, at, pl.ds(BLOCK + lane, 128)] = imag.astype(jnp.bfloat16)

    def fold_circle(circle, carry):
        probe_copy(circle).wait()

        @pl.when(circle == 1)
        def _():
            table_copy.start()

        fold(circle, 0)
        fold(circle, 1)
        return carry

    lax.fori_loop(0, circles, fold_circle, 0)
    table_copy.wait()
    for side in range(2):
        for c in range(HALF):
            j = c + side
            depth = BLOCK if j in (0, HALF) else 2 * BLOCK
            coef = dot(y_ref[j, :, :depth], table_ref[side, c, :depth, :]).astype(jnp.bfloat16)
            for group in range(groups):
                for part in range(2):
                    base = group * 4 * rows + (2 * side + part) * rows
                    four_ref[base : base + rows, c * WAVES : (c + 1) * WAVES] = coef[
                        group * rows : (group + 1) * rows, part * WAVES : (part + 1) * WAVES
                    ]
    items = wide_ref.shape[0]
    for first in range(0, circles, 2):
        last = min(first + 2, circles)
        moved = dot(pick_ref[...], four_ref[first * width : last * width, :], NT)
        for t in range(first, last):
            for item in range(items):
                wide_ref[item, pl.ds(t, devices, stride=8), :] = moved[
                    item * devices : (item + 1) * devices,
                    (t - first) * width : (t - first + 1) * width,
                ]
    copies = []
    for item in range(items):
        send_ref[item] = wide_ref[item].astype(jnp.bfloat16)
        copy = pltpu.make_async_copy(
            send_ref.at[item], out_hbm.at[:, pl.ds(item * width, width)], out_sem.at[item]
        )
        copy.start()
        copies.append(copy)
    for copy in copies:
        copy.wait()


def legendre_kernel(
    pair_ref,
    coming_ref,
    table_hbm,
    row_ref,
    order_ref,
    out_hbm,
    table_ref,
    x_ref,
    b_ref,
    pick_ref,
    back_ref,
    wide_ref,
    send_ref,
    table_sem,
    out_sem,
):
    items, width, circle_half = x_ref.shape
    degrees = table_ref.shape[1] - 1
    half_width = width // 2
    quarter = width // 4
    slots = coming_ref.shape[0]
    devices = slots // 8
    circles = wide_ref.shape[0]

    spans = [(first, min(first + 2, items)) for first in range(0, items, 2)]


    def table_copy(i):
        return pltpu.make_async_copy(table_hbm.at[i], table_ref.at[i], table_sem.at[i])

    for i in range(3):
        table_copy(i).start()
    where = lax.broadcasted_iota(jnp.int32, (circle_half, slots), 0)
    pick_ref[...] = jnp.where(row_ref[...] == where, 1.0, 0.0).astype(jnp.bfloat16)
    for first, last in spans:
        natural = dot(pick_ref[...], coming_ref[:, first * width : last * width])
        for i in range(first, last):
            x = natural[:, (i - first) * width : (i - first + 1) * width].astype(jnp.bfloat16).T
            north, south = x[:half_width].astype(jnp.float32), x[half_width:].astype(jnp.float32)
            x_ref[i, :half_width] = (north + south).astype(jnp.bfloat16)
            x_ref[i, half_width:] = (north - south).astype(jnp.bfloat16)
    mark_rows(back_ref, order_ref[...].astype(jnp.float32))
    for t in range(circles):
        wide_ref[t, pl.ds(7, devices, stride=8), :] = jnp.zeros((devices, width), jnp.float32)

    for i in range(items):
        q = pair_ref[i]
        swap = (q % RADIX >= HALF).astype(jnp.int32)

        def weights(first, length):
            row = lax.broadcasted_iota(jnp.int32, (1, length), 1) + first
            second = row >= degrees - q
            degree = jnp.where(second, row - 1, q + row).astype(jnp.float32)
            damping = 1.0 / (1.0 + 4.0 * degree * (degree + 1.0) / float(degrees * degrees))
            wave = second.astype(jnp.int32) ^ swap
            parity = jnp.where(second, row + q, row) & 1
            code = 2 * parity + wave
            return [jnp.where(code == k, damping, 0.0) for k in range(4)]

        main_weights = weights(0, degrees)
        last_weights = weights(degrees, 1)
        table_copy(i).wait()
        if i + 3 < items:
            table_copy(i + 3).start()
        spectrum = dot(x_ref[i], table_ref[i, :degrees, :], NT)
        last_row = table_ref[i, degrees:, :].astype(jnp.float32)
        last = jnp.sum(x_ref[i].astype(jnp.float32) * last_row, axis=1, keepdims=True)
        scaled = jnp.concatenate(
            [
                (spectrum[k * quarter : (k + 1) * quarter] * main_weights[k]).astype(jnp.bfloat16)
                for k in range(4)
            ],
            axis=0,
        )
        scaled_last = jnp.concatenate(
            [
                (last[k * quarter : (k + 1) * quarter] * last_weights[k])
                .astype(jnp.bfloat16)
                .astype(jnp.float32)
                for k in range(4)
            ],
            axis=0,
        )
        total = dot(scaled, table_ref[i, :degrees, :])
        total = total + scaled_last * last_row
        even, odd = total[:half_width], total[half_width:]
        b_ref[i * width : i * width + half_width, :] = (even + odd).astype(jnp.bfloat16)
        b_ref[i * width + half_width : (i + 1) * width, :] = (even - odd).astype(jnp.bfloat16)

    for first, last in spans:
        moved = dot(back_ref[...], b_ref[first * width : last * width, :], NT)
        for i in range(first, last):
            for t in range(circles):
                wide_ref[t, pl.ds(i, devices, stride=8), :] = moved[
                    t * devices : (t + 1) * devices, (i - first) * width : (i - first + 1) * width
                ]
    copies = []
    for t in range(circles):
        send_ref[t] = wide_ref[t].astype(jnp.bfloat16)
        copy = pltpu.make_async_copy(
            send_ref.at[t], out_hbm.at[:, pl.ds(t * width, width)], out_sem.at[t]
        )
        copy.start()
        copies.append(copy)
    for copy in copies:
        copy.wait()


def synthesise_kernel(
    coming_ref,
    kappa_hbm,
    table_hbm,
    pair_ref,
    out_hbm,
    kappa_ref,
    table_ref,
    pick_ref,
    turned_ref,
    left_ref,
    u_ref,
    filt_ref,
    kappa_sem,
    table_sem,
    out_sem,
):
    rows = filt_ref.shape[1]
    circles = kappa_ref.shape[0]
    width = 8 * rows
    reps = pick_ref.shape[1]

    kappa_copy = pltpu.make_async_copy(kappa_hbm, kappa_ref, kappa_sem)
    kappa_copy.start()
    table_copy = pltpu.make_async_copy(table_hbm, table_ref, table_sem)
    table_copy.start()
    mark_rows(pick_ref, representative(pair_ref[...].astype(jnp.float32)))
    for t in range(circles):
        turned_ref[t * width : (t + 1) * width, :] = coming_ref[:, t * width : (t + 1) * width].T
    for first in range(0, HALF, 2):
        last = min(first + 2, HALF)
        coef = dot(turned_ref[...], pick_ref[:, first * WAVES : last * WAVES]).astype(jnp.bfloat16)
        for t in range(circles):
            for side in range(2):
                group = 2 * t + side
                for part in range(4):
                    base = t * width + side * 4 * rows + part * rows
                    for c in range(first, last):
                        left_ref[
                            c + part // 2,
                            group * rows : (group + 1) * rows,
                            part * WAVES : (part + 1) * WAVES,
                        ] = coef[base : base + rows, (c - first) * WAVES : (c - first + 1) * WAVES]
    table_copy.wait()
    two = 2 * WAVES
    for j in range(HALF + 1):
        if j == 0:
            u_ref[j, :, :BLOCK] = dot(left_ref[j, :, :two], table_ref[0, 0, :, :BLOCK])
        elif j == HALF:
            u_ref[j, :, :BLOCK] = dot(left_ref[j, :, two:], table_ref[1, j - 1, :, :BLOCK])
        else:
            u_ref[j] = dot(left_ref[j, :, :two], table_ref[0, j]) + dot(
                left_ref[j, :, two:], table_ref[1, j - 1]
            )
    kappa_copy.wait()

    def unfold(circle, side):
        group = 2 * circle + side
        at = pl.ds(pl.multiple_of(group * rows, rows), rows)
        for lane in range(0, BLOCK, 128):
            real = [u_ref[j, at, pl.ds(lane, 128)] for j in range(HALF + 1)]
            imag = [None] + [u_ref[j, at, pl.ds(BLOCK + lane, 128)] for j in range(1, HALF)]
            value = [None] * RADIX
            for b in range(4):
                cos_even = real[0]
                for j in (2, 4, 6):
                    cos_even = cos_even + real[j] * ring(j * b)[0]
                cos_odd = real[HALF] * ring(HALF * b)[0]
                for j in (1, 3, 5):
                    cos_odd = cos_odd + real[j] * ring(j * b)[0]
                if b == 0:
                    value[0] = cos_even + cos_odd
                    value[HALF] = cos_even - cos_odd
                    continue
                sin_even = imag[2] * ring(2 * b)[1]
                for j in (4, 6):
                    sin_even = sin_even + imag[j] * ring(j * b)[1]
                sin_odd = imag[1] * ring(b)[1]
                for j in (3, 5):
                    sin_odd = sin_odd + imag[j] * ring(j * b)[1]
                up, down = cos_even + cos_odd, cos_even - cos_odd
                sup, sdown = sin_even + sin_odd, sin_even - sin_odd
                value[b] = up - sup
                value[RADIX - b] = up + sup
                value[HALF + b] = down - sdown
                value[HALF - b] = down + sdown
            for b in range(RADIX):
                cut = pl.ds(b * BLOCK + lane, 128)
                scale = kappa_ref[circle, side : side + 1, cut]
                filt_ref[group, :, cut] = (value[b] * scale).astype(jnp.bfloat16)

    def out_copy(circle):
        return pltpu.make_async_copy(
            filt_ref.at[pl.ds(2 * circle, 2)], out_hbm.at[pl.ds(2 * circle, 2)], out_sem.at[circle]
        )

    def unfold_circle(circle, carry):
        unfold(circle, 0)
        unfold(circle, 1)
        out_copy(circle).start()
        return carry

    lax.fori_loop(0, circles, unfold_circle, 0)
    for t in range(circles):
        out_copy(t).wait()


VMEM = pl.BlockSpec(memory_space=pltpu.VMEM)
SMEM = pl.BlockSpec(memory_space=pltpu.SMEM)
ANY = pl.BlockSpec(memory_space=pl.ANY)
HBM = pl.BlockSpec(memory_space=pltpu.HBM)
NOWHERE = 10000


def stay(array):
    return pltpu.with_memory_space_constraint(array, pltpu.HBM)


def near(array):
    return pltpu.with_memory_space_constraint(array, pltpu.VMEM)


def limit(mib):
    return pltpu.CompilerParams(vmem_limit_bytes=mib * 2**20)


def per_device(probe_field, kappa_field, circle_order, pair_order, legendre_table):
    circles, sides, probes, longitudes = probe_field.shape
    items, row_count, circle_half = legendre_table.shape
    devices = lax.axis_size(AXES)
    groups = circles * sides
    reps = HALF * WAVES
    width = 8 * probes
    slots = devices * 8
    ahead, back = fourier_tables(longitudes)
    ahead, back = jnp.asarray(ahead), jnp.asarray(back)

    def by_device(order, count):
        held = order.reshape(devices, count)
        return jnp.pad(held, ((0, 0), (0, 8 - count)), constant_values=NOWHERE).reshape(1, slots)

    def by_place(order, count):
        return order.reshape(devices, count).T.reshape(1, count * devices)

    def swap_over(payload):
        blocks = payload.reshape(devices, 8, payload.shape[1])
        moved = lax.all_to_all(blocks, AXES, split_axis=0, concat_axis=0, tiled=True)
        return moved.reshape(payload.shape)

    bf16, f32 = jnp.bfloat16, jnp.float32
    dma = pltpu.SemaphoreType.DMA
    sending = pl.pallas_call(
        analyse_kernel,
        out_shape=pltpu.HBM((slots, items * width), bf16),
        in_specs=[HBM, HBM, HBM, VMEM],
        out_specs=HBM,
        scratch_shapes=[
            pltpu.VMEM((groups, probes, longitudes), bf16),
            pltpu.VMEM(kappa_field.shape, f32),
            pltpu.VMEM(ahead.shape, bf16),
            pltpu.VMEM((HALF + 1, groups * probes, 2 * BLOCK), bf16),
            pltpu.VMEM((circles * width, reps), bf16),
            pltpu.VMEM((items * devices, reps), bf16),
            pltpu.VMEM((items, slots, width), f32),
            pltpu.VMEM((items, slots, width), bf16),
            dma((circles,)),
            dma,
            dma,
            dma((items,)),
        ],
        compiler_params=limit(40),
        name="analyse",
    )(
        stay(probe_field.reshape(groups, probes, longitudes)),
        stay(kappa_field),
        stay(ahead),
        by_place(pair_order, items),
    )
    coming = swap_over(sending)

    pairs = lax.dynamic_slice(pair_order, (lax.axis_index(AXES) * items,), (items,))
    sending = pl.pallas_call(
        legendre_kernel,
        out_shape=pltpu.HBM((slots, circles * width), bf16),
        in_specs=[SMEM, VMEM, HBM, VMEM, VMEM],
        out_specs=HBM,
        scratch_shapes=[
            pltpu.VMEM((items, row_count, circle_half), bf16),
            pltpu.VMEM((items, width, circle_half), bf16),
            pltpu.VMEM((items * width, circle_half), bf16),
            pltpu.VMEM((circle_half, slots), bf16),
            pltpu.VMEM((circles * devices, circle_half), bf16),
            pltpu.VMEM((circles, slots, width), f32),
            pltpu.VMEM((circles, slots, width), bf16),
            dma((items,)),
            dma((circles,)),
        ],
        compiler_params=limit(48),
        name="legendre",
    )(
        pairs,
        near(coming),
        stay(legendre_table),
        by_device(circle_order, circles),
        by_place(circle_order, circles),
    )
    coming = swap_over(sending)

    filtered = pl.pallas_call(
        synthesise_kernel,
        out_shape=jax.ShapeDtypeStruct((groups, probes, longitudes), bf16),
        in_specs=[VMEM, HBM, HBM, VMEM],
        out_specs=HBM,
        scratch_shapes=[
            pltpu.VMEM(kappa_field.shape, f32),
            pltpu.VMEM(back.shape, bf16),
            pltpu.VMEM((slots, reps), bf16),
            pltpu.VMEM((circles * width, slots), bf16),
            pltpu.VMEM((HALF + 1, groups * probes, 4 * WAVES), bf16),
            pltpu.VMEM((HALF + 1, groups * probes, 2 * BLOCK), f32),
            pltpu.VMEM((groups, probes, longitudes), bf16),
            dma,
            dma,
            dma((circles,)),
        ],
        compiler_params=limit(40),
        name="synthesise",
    )(
        near(coming), stay(kappa_field), stay(back), by_device(pair_order, items)
    )
    return filtered.reshape(circles, sides, probes, longitudes)


def solution(mesh):
    return jax.shard_map(
        per_device,
        mesh=mesh,
        in_specs=(
            P(AXES, None, None, None),
            P(AXES, None, None),
            P(),
            P(),
            P(AXES, None, None),
        ),
        out_specs=P(AXES, None, None, None),
        check_vma=False,
    )
```

time: 116 us -> 104 us (0.90)
  Pallas kernels: 41.2 us -> 32 us
  local copies, waits for them, and re-layouts: 8.08 us -> 2.22 us
  waiting for transfers between devices: 49.7 us -> 52.6 us
    pallas_call x2, Pallas kernels: 33.1 us -> 26.9 us  [the longest x1 18.8 us: per_device(): pl.pallas_call(legendre_kernel, out_shape=pltpu.HBM((slots, circles * wid...]
    unnamed x10 -> x4, local copies, waits for them, and re-layouts: 4.53 us -> 0.02 us
    pallas_call x1, Pallas kernels: 8.07 us -> 5.1 us  [per_device(): pl.pallas_call(synthesise_kernel, out_shape=jax.ShapeDtypeStruct((groups,...]
    all_to_all x2, waiting for transfers between devices: 49.7 us -> 52.6 us  [swap_over(): lax.all_to_all(blocks, AXES, split_axis=0, concat_axis=0, tiled=True)]
  transfers between devices with their start and end apart: 2 -> 2, of which waited for: 2 -> 2; matrix products, arithmetic and copies ran while one was open for 4% -> 1% of each run, Pallas kernels for 0% -> 0%
where the time goes in v2:
time: 104 us; the launch traced here: 103 us
  waiting for transfers between devices  52.6 us (51%)
  Pallas kernels  32 us (31%)
  starting transfers between devices  16.3 us (16%)
  local copies, waits for them, and re-layouts  2.22 us (2%)
    all_to_all x2, waiting for transfers between devices, swap_over(): lax.all_to_all(blocks, AXES, split_axis=0, concat_axis=0, tiled=True)  52.6 us
    pallas_call x1, Pallas kernels, per_device(): pl.pallas_call(legendre_kernel, out_shape=pltpu.HBM((slots, circles * wid...  18.8 us
    all_to_all x2, starting transfers between devices, swap_over(): lax.all_to_all(blocks, AXES, split_axis=0, concat_axis=0, tiled=True)  16.3 us
    pallas_call x1, Pallas kernels, per_device(): pl.pallas_call(analyse_kernel, out_shape=pltpu.HBM((slots, items * width)...  8.13 us
    pallas_call x1, Pallas kernels, per_device(): pl.pallas_call(synthesise_kernel, out_shape=jax.ShapeDtypeStruct((groups,...  5.1 us
  transfers between devices with their start and end apart: 2, of which 2 were waited for; matrix products, arithmetic and copies ran while one was open for 1% of the time, Pallas kernels for 0%

profile of v2, /device:TPU:1, one launch (start us, length us, event | category | flops | bytes accessed | tf_op | source)
XLA Modules:
  0.0 103.4 jit_solution(1804063433990781025)
XLA Ops:
  0.0 0.9 reshape.39
  0.9 0.1 copy.10
  1.0 8.1 %analyse.1 = bf16[1024,896]{1,0:T(8,128)(2,1)} custom-call(bf16[14,16,3584]{2,1,0:T(8,128)(2,1)} %bitcast.24, f32[7,2,3584]{2,1,0:T(2,128)} %kappa_hbm.3, bf16[2,7,512,256]{3,2,1,0:T(8,128)(2,1)} %constant.23.clone.table_hbm, s32[1,896]{1,0:T(1,128)S(1)} %bitcast.21), custom_call_target="tpu_custom_call" | custom-call | tf_op jit(solution)/shard_map/analyse/pallas_call | solution.py:458
  9.1 0.0 copy-start
  9.1 11.7 %all-to-all-start = ((bf16[128,8,896]{2,1,0:T(8,128)(2,1)}), bf16[128,8,896]{2,1,0:T(8,128)(2,1)S(1)}, u32[]{:S(2)}, u32[]{:S(2)}) async-start(bf16[128,8,896]{2,1,0:T(8,128)(2,1)} %bitcast.23), calls=%async_computation | async-start | bytes 3670016 | tf_op jit(solution)/shard_map/all_to_all | solution.py:453
  20.8 0.8 dynamic_slice.3.pair_ref
  21.6 0.0 copy-done
  21.6 0.2 reshape.43
  21.8 0.1 copy.11
  21.9 0.1 reshape.44.row_ref
  22.0 25.6 %all-to-all-done = bf16[128,8,896]{2,1,0:T(8,128)(2,1)S(1)} async-done(((bf16[128,8,896]{2,1,0:T(8,128)(2,1)}), bf16[128,8,896]{2,1,0:T(8,128)(2,1)S(1)}, u32[]{:S(2)}, u32[]{:S(2)}) %all-to-all-start) | async-done | bytes 1835040 | tf_op jit(solution)/shard_map/all_to_all | solution.py:453
  47.6 18.8 %legendre.1 = bf16[1024,896]{1,0:T(8,128)(2,1)} custom-call(s32[7]{0:T(128)S(1)} %dynamic_slice.3.pair_ref, bf16[1024,896]{1,0:T(8,128)(2,1)S(1)} %bitcast.18, bf16[7,1793,896]{2,1,0:T(8,128)(2,1)} %table_hbm.3, s32[1,1024]{1,0:T(1,128)S(1)} %reshape.44.row_ref, s32[1,896]{1,0:T(1,128)S(1)} %bitcast.20), custom_call_target="tpu_custom_call" | custom-call | tf_op jit(solution)/shard_map/legendre/pallas_call | solution.py:488
  66.4 4.6 %all-to-all-start.1 = ((bf16[128,8,896]{2,1,0:T(8,128)(2,1)}), bf16[128,8,896]{2,1,0:T(8,128)(2,1)S(1)}, u32[]{:S(2)}, u32[]{:S(2)}) async-start(bf16[128,8,896]{2,1,0:T(8,128)(2,1)} %bitcast.22), calls=%async_computation.1 | async-start | bytes 3670016 | tf_op jit(solution)/shard_map/all_to_all | solution.py:453
  71.0 0.1 reshape.48.pair_ref
  71.1 27.0 %all-to-all-done.1 = bf16[128,8,896]{2,1,0:T(8,128)(2,1)S(1)} async-done(((bf16[128,8,896]{2,1,0:T(8,128)(2,1)}), bf16[128,8,896]{2,1,0:T(8,128)(2,1)S(1)}, u32[]{:S(2)}, u32[]{:S(2)}) %all-to-all-start.1) | async-done | bytes 1835040 | tf_op jit(solution)/shard_map/all_to_all | solution.py:453
  98.1 5.1 %synthesise.1 = bf16[14,16,3584]{2,1,0:T(8,128)(2,1)} custom-call(bf16[1024,896]{1,0:T(8,128)(2,1)S(1)} %bitcast.19, f32[7,2,3584]{2,1,0:T(2,128)} %kappa_hbm.3, bf16[2,7,256,512]{3,2,1,0:T(8,128)(2,1)} %constant.24.clone.table_hbm, s32[1,1024]{1,0:T(1,128)S(1)} %reshape.48.pair_ref), custom_call_target="tpu_custom_call" | custom-call | tf_op jit(solution)/shard_map/synthesise/pallas_call | solution.py:515
  (4 shorter events, 0.1 us)
Async XLA Ops:
  9.1 12.5 %copy-start = (s32[896]{0:T(1024)S(1)}, s32[896]{0:T(1024)}, u32[]{:S(2)}) copy-start(s32[896]{0:T(1024)} %param.9) | copy-start | bytes 10756
  9.1 38.5 %all-to-all-start = ((bf16[128,8,896]{2,1,0:T(8,128)(2,1)}), bf16[128,8,896]{2,1,0:T(8,128)(2,1)S(1)}, u32[]{:S(2)}, u32[]{:S(2)}) async-start(bf16[128,8,896]{2,1,0:T(8,128)(2,1)} %bitcast.23), calls=%async_computation | async-start | bytes 3670016 | tf_op jit(solution)/shard_map/all_to_all | solution.py:453
  66.4 31.7 %all-to-all-start.1 = ((bf16[128,8,896]{2,1,0:T(8,128)(2,1)}), bf16[128,8,896]{2,1,0:T(8,128)(2,1)S(1)}, u32[]{:S(2)}, u32[]{:S(2)}) async-start(bf16[128,8,896]{2,1,0:T(8,128)(2,1)} %bitcast.22), calls=%async_computation.1 | async-start | bytes 3670016 | tf_op jit(solution)/shard_map/all_to_all | solution.py:453

commit v3 on v2

--- a/solution.py
+++ b/solution.py
@@ -110,7 +110,10 @@
     kappa_copy.start()
     for t in range(circles):
         probe_copy(t).start()
-    table_copy = pltpu.make_async_copy(table_hbm, table_ref, table_sem)
+
+    def table_copy(side):
+        return pltpu.make_async_copy(table_hbm.at[side], table_ref.at[side], table_sem.at[side])
+
     mark_rows(pick_ref, representative(pair_ref[...].astype(jnp.float32)))
     for t in range(circles):
         wide_ref[t, pl.ds(7, devices, stride=8), :] = jnp.zeros((devices, width), jnp.float32)
@@ -152,17 +155,18 @@
     def fold_circle(circle, carry):
         probe_copy(circle).wait()
 
-        @pl.when(circle == 1)
+        @pl.when(circle == 0)
         def _():
-            table_copy.start()
+            table_copy(0).start()
+            table_copy(1).start()
 
         fold(circle, 0)
         fold(circle, 1)
         return carry
 
     lax.fori_loop(0, circles, fold_circle, 0)
-    table_copy.wait()
     for side in range(2):
+        table_copy(side).wait()
         for c in range(HALF):
             j = c + side
             depth = BLOCK if j in (0, HALF) else 2 * BLOCK
@@ -471,7 +475,7 @@
             pltpu.VMEM((items, slots, width), bf16),
             dma((circles,)),
             dma,
-            dma,
+            dma((2,)),
             dma((items,)),
         ],
         compiler_params=limit(40),

time: 104 us -> 103 us (level)
  no operation moved by 1% of the time
where the time goes in v3:
time: 103 us
  waiting for transfers between devices  52.6 us (51%)
  Pallas kernels  31.5 us (31%)
  starting transfers between devices  16.3 us (16%)
  local copies, waits for them, and re-layouts  2.22 us (2%)
    all_to_all x2, waiting for transfers between devices, swap_over(): lax.all_to_all(blocks, AXES, split_axis=0, concat_axis=0, tiled=True)  52.6 us
    pallas_call x1, Pallas kernels, per_device(): pl.pallas_call(legendre_kernel, out_shape=pltpu.HBM((slots, circles * wid...  18.8 us
    all_to_all x2, starting transfers between devices, swap_over(): lax.all_to_all(blocks, AXES, split_axis=0, concat_axis=0, tiled=True)  16.3 us
    pallas_call x1, Pallas kernels, per_device(): pl.pallas_call(analyse_kernel, out_shape=pltpu.HBM((slots, items * width)...  7.63 us
    pallas_call x1, Pallas kernels, per_device(): pl.pallas_call(synthesise_kernel, out_shape=jax.ShapeDtypeStruct((groups,...  5.1 us
  transfers between devices with their start and end apart: 2, of which 2 were waited for; matrix products, arithmetic and copies ran while one was open for 1% of the time, Pallas kernels for 0%

profile of v3, /device:TPU:1, one launch (start us, length us, event | category | flops | bytes accessed | tf_op | source)
XLA Modules:
  0.0 102.9 jit_solution(18275725907758754967)
XLA Ops:
  0.0 0.9 reshape.39
  0.9 0.1 copy.10
  1.0 7.6 %analyse.1 = bf16[1024,896]{1,0:T(8,128)(2,1)} custom-call(bf16[14,16,3584]{2,1,0:T(8,128)(2,1)} %bitcast.24, f32[7,2,3584]{2,1,0:T(2,128)} %kappa_hbm.3, bf16[2,7,512,256]{3,2,1,0:T(8,128)(2,1)} %constant.23.clone.table_hbm, s32[1,896]{1,0:T(1,128)S(1)} %bitcast.21), custom_call_target="tpu_custom_call" | custom-call | tf_op jit(solution)/shard_map/analyse/pallas_call | solution.py:462
  8.6 0.0 copy-start
  8.6 11.7 %all-to-all-start = ((bf16[128,8,896]{2,1,0:T(8,128)(2,1)}), bf16[128,8,896]{2,1,0:T(8,128)(2,1)S(1)}, u32[]{:S(2)}, u32[]{:S(2)}) async-start(bf16[128,8,896]{2,1,0:T(8,128)(2,1)} %bitcast.23), calls=%async_computation | async-start | bytes 3670016 | tf_op jit(solution)/shard_map/all_to_all | solution.py:457
  20.3 0.8 dynamic_slice.3.pair_ref
  21.1 0.0 copy-done
  21.1 0.2 reshape.43
  21.3 0.1 copy.11
  21.4 0.1 reshape.44.row_ref
  21.5 25.6 %all-to-all-done = bf16[128,8,896]{2,1,0:T(8,128)(2,1)S(1)} async-done(((bf16[128,8,896]{2,1,0:T(8,128)(2,1)}), bf16[128,8,896]{2,1,0:T(8,128)(2,1)S(1)}, u32[]{:S(2)}, u32[]{:S(2)}) %all-to-all-start) | async-done | bytes 1835040 | tf_op jit(solution)/shard_map/all_to_all | solution.py:457
  47.1 18.8 %legendre.1 = bf16[1024,896]{1,0:T(8,128)(2,1)} custom-call(s32[7]{0:T(128)S(1)} %dynamic_slice.3.pair_ref, bf16[1024,896]{1,0:T(8,128)(2,1)S(1)} %bitcast.18, bf16[7,1793,896]{2,1,0:T(8,128)(2,1)} %table_hbm.3, s32[1,1024]{1,0:T(1,128)S(1)} %reshape.44.row_ref, s32[1,896]{1,0:T(1,128)S(1)} %bitcast.20), custom_call_target="tpu_custom_call" | custom-call | tf_op jit(solution)/shard_map/legendre/pallas_call | solution.py:492
  65.9 4.6 %all-to-all-start.1 = ((bf16[128,8,896]{2,1,0:T(8,128)(2,1)}), bf16[128,8,896]{2,1,0:T(8,128)(2,1)S(1)}, u32[]{:S(2)}, u32[]{:S(2)}) async-start(bf16[128,8,896]{2,1,0:T(8,128)(2,1)} %bitcast.22), calls=%async_computation.1 | async-start | bytes 3670016 | tf_op jit(solution)/shard_map/all_to_all | solution.py:457
  70.5 0.1 reshape.48.pair_ref
  70.6 27.0 %all-to-all-done.1 = bf16[128,8,896]{2,1,0:T(8,128)(2,1)S(1)} async-done(((bf16[128,8,896]{2,1,0:T(8,128)(2,1)}), bf16[128,8,896]{2,1,0:T(8,128)(2,1)S(1)}, u32[]{:S(2)}, u32[]{:S(2)}) %all-to-all-start.1) | async-done | bytes 1835040 | tf_op jit(solution)/shard_map/all_to_all | solution.py:457
  97.6 5.1 %synthesise.1 = bf16[14,16,3584]{2,1,0:T(8,128)(2,1)} custom-call(bf16[1024,896]{1,0:T(8,128)(2,1)S(1)} %bitcast.19, f32[7,2,3584]{2,1,0:T(2,128)} %kappa_hbm.3, bf16[2,7,256,512]{3,2,1,0:T(8,128)(2,1)} %constant.24.clone.table_hbm, s32[1,1024]{1,0:T(1,128)S(1)} %reshape.48.pair_ref), custom_call_target="tpu_custom_call" | custom-call | tf_op jit(solution)/shard_map/synthesise/pallas_call | solution.py:519
  (4 shorter events, 0.1 us)
Async XLA Ops:
  8.6 12.5 %copy-start = (s32[896]{0:T(1024)S(1)}, s32[896]{0:T(1024)}, u32[]{:S(2)}) copy-start(s32[896]{0:T(1024)} %param.9) | copy-start | bytes 10756
  8.6 38.5 %all-to-all-start = ((bf16[128,8,896]{2,1,0:T(8,128)(2,1)}), bf16[128,8,896]{2,1,0:T(8,128)(2,1)S(1)}, u32[]{:S(2)}, u32[]{:S(2)}) async-start(bf16[128,8,896]{2,1,0:T(8,128)(2,1)} %bitcast.23), calls=%async_computation | async-start | bytes 3670016 | tf_op jit(solution)/shard_map/all_to_all | solution.py:457
  65.9 31.7 %all-to-all-start.1 = ((bf16[128,8,896]{2,1,0:T(8,128)(2,1)}), bf16[128,8,896]{2,1,0:T(8,128)(2,1)S(1)}, u32[]{:S(2)}, u32[]{:S(2)}) async-start(bf16[128,8,896]{2,1,0:T(8,128)(2,1)} %bitcast.22), calls=%async_computation.1 | async-start | bytes 3670016 | tf_op jit(solution)/shard_map/all_to_all | solution.py:457

commit v4 on v3

--- a/solution.py
+++ b/solution.py
@@ -90,6 +90,7 @@
     pick_ref,
     wide_ref,
     send_ref,
+    upright_ref,
     probe_sem,
     kappa_sem,
     table_sem,
@@ -114,7 +115,17 @@
     def table_copy(side):
         return pltpu.make_async_copy(table_hbm.at[side], table_ref.at[side], table_sem.at[side])
 
-    mark_rows(pick_ref, representative(pair_ref[...].astype(jnp.float32)))
+    rep = representative(pair_ref[...].astype(jnp.float32))
+    for r in range(rep.shape[0]):
+        upright_ref[r * devices : (r + 1) * devices, :] = column(rep[r : r + 1])
+    lanes = lax.broadcasted_iota(jnp.int32, (devices, WAVES), 1).astype(jnp.float32)
+    for item in range(rep.shape[0]):
+        upright = upright_ref[pl.ds(item, devices, stride=rep.shape[0]), :]
+        for start in range(0, reps, WAVES):
+            hit = jnp.where(upright == lanes + float(start), 1.0, 0.0)
+            pick_ref[item * devices : (item + 1) * devices, start : start + WAVES] = hit.astype(
+                jnp.bfloat16
+            )
     for t in range(circles):
         wide_ref[t, pl.ds(7, devices, stride=8), :] = jnp.zeros((devices, width), jnp.float32)
     kappa_copy.wait()
@@ -473,6 +484,7 @@
             pltpu.VMEM((items * devices, reps), bf16),
             pltpu.VMEM((items, slots, width), f32),
             pltpu.VMEM((items, slots, width), bf16),
+            pltpu.VMEM((items * devices, WAVES), f32),
             dma((circles,)),
             dma,
             dma((2,)),
@@ -484,7 +496,7 @@
         stay(probe_field.reshape(groups, probes, longitudes)),
         stay(kappa_field),
         stay(ahead),
-        by_place(pair_order, items),
+        pair_order.reshape(items, devices),
     )
     coming = swap_over(sending)
 

time: 103 us -> 103 us (level)
  no operation moved by 1% of the time
where the time goes in v4:
time: 103 us; the launch traced here: 102 us
  waiting for transfers between devices  53.1 us (52%)
  Pallas kernels  31.4 us (30%)
  starting transfers between devices  16.3 us (16%)
  local copies, waits for them, and re-layouts  1.45 us (1%)
    all_to_all x2, waiting for transfers between devices, swap_over(): lax.all_to_all(blocks, AXES, split_axis=0, concat_axis=0, tiled=True)  53.1 us
    pallas_call x1, Pallas kernels, per_device(): pl.pallas_call(legendre_kernel, out_shape=pltpu.HBM((slots, circles * wid...  18.7 us
    all_to_all x2, starting transfers between devices, swap_over(): lax.all_to_all(blocks, AXES, split_axis=0, concat_axis=0, tiled=True)  16.3 us
    pallas_call x1, Pallas kernels, per_device(): pl.pallas_call(analyse_kernel, out_shape=pltpu.HBM((slots, items * width)...  7.52 us
    pallas_call x1, Pallas kernels, per_device(): pl.pallas_call(synthesise_kernel, out_shape=jax.ShapeDtypeStruct((groups,...  5.11 us
  transfers between devices with their start and end apart: 2, of which 2 were waited for; matrix products, arithmetic and copies ran while one was open for 1% of the time, Pallas kernels for 0%

profile of v4, /device:TPU:1, one launch (start us, length us, event | category | flops | bytes accessed | tf_op | source)
XLA Modules:
  0.0 102.5 jit_solution(13338964610954166886)
XLA Ops:
  0.0 0.0 copy-start
  0.0 0.7 copy-done
  0.7 7.5 %analyse.1 = bf16[1024,896]{1,0:T(8,128)(2,1)} custom-call(bf16[14,16,3584]{2,1,0:T(8,128)(2,1)} %bitcast.19, f32[7,2,3584]{2,1,0:T(2,128)} %kappa_hbm.3, bf16[2,7,512,256]{3,2,1,0:T(8,128)(2,1)} %constant.23.clone.table_hbm, s32[7,128]{1,0:T(8,128)S(1)} %bitcast.15), custom_call_target="tpu_custom_call" | custom-call | tf_op jit(solution)/shard_map/analyse/pallas_call | solution.py:473
  8.2 0.0 copy-start.1
  8.2 0.0 copy-start.2
  8.2 11.7 %all-to-all-start = ((bf16[128,8,896]{2,1,0:T(8,128)(2,1)}), bf16[128,8,896]{2,1,0:T(8,128)(2,1)S(1)}, u32[]{:S(2)}, u32[]{:S(2)}) async-start(bf16[128,8,896]{2,1,0:T(8,128)(2,1)} %bitcast.18), calls=%async_computation | async-start | bytes 3670016 | tf_op jit(solution)/shard_map/all_to_all | solution.py:468
  19.9 0.0 copy-done.1
  19.9 0.1 dynamic_slice.3.pair_ref
  20.0 0.0 copy-done.2
  20.0 0.2 reshape.41
  20.2 0.1 reshape.42.row_ref
  20.3 0.1 copy.9
  20.4 26.3 %all-to-all-done = bf16[128,8,896]{2,1,0:T(8,128)(2,1)S(1)} async-done(((bf16[128,8,896]{2,1,0:T(8,128)(2,1)}), bf16[128,8,896]{2,1,0:T(8,128)(2,1)S(1)}, u32[]{:S(2)}, u32[]{:S(2)}) %all-to-all-start) | async-done | bytes 1835040 | tf_op jit(solution)/shard_map/all_to_all | solution.py:468
  46.7 18.7 %legendre.1 = bf16[1024,896]{1,0:T(8,128)(2,1)} custom-call(s32[7]{0:T(128)S(1)} %dynamic_slice.3.pair_ref, bf16[1024,896]{1,0:T(8,128)(2,1)S(1)} %bitcast.13, bf16[7,1793,896]{2,1,0:T(8,128)(2,1)} %table_hbm.3, s32[1,1024]{1,0:T(1,128)S(1)} %reshape.42.row_ref, s32[1,896]{1,0:T(1,128)S(1)} %bitcast.16), custom_call_target="tpu_custom_call" | custom-call | tf_op jit(solution)/shard_map/legendre/pallas_call | solution.py:504
  65.4 4.6 %all-to-all-start.1 = ((bf16[128,8,896]{2,1,0:T(8,128)(2,1)}), bf16[128,8,896]{2,1,0:T(8,128)(2,1)S(1)}, u32[]{:S(2)}, u32[]{:S(2)}) async-start(bf16[128,8,896]{2,1,0:T(8,128)(2,1)} %bitcast.17), calls=%async_computation.1 | async-start | bytes 3670016 | tf_op jit(solution)/shard_map/all_to_all | solution.py:468
  70.1 0.2 reshape.46
  70.3 0.1 reshape.47.pair_ref
  70.4 26.8 %all-to-all-done.1 = bf16[128,8,896]{2,1,0:T(8,128)(2,1)S(1)} async-done(((bf16[128,8,896]{2,1,0:T(8,128)(2,1)}), bf16[128,8,896]{2,1,0:T(8,128)(2,1)S(1)}, u32[]{:S(2)}, u32[]{:S(2)}) %all-to-all-start.1) | async-done | bytes 1835040 | tf_op jit(solution)/shard_map/all_to_all | solution.py:468
  97.2 5.1 %synthesise.1 = bf16[14,16,3584]{2,1,0:T(8,128)(2,1)} custom-call(bf16[1024,896]{1,0:T(8,128)(2,1)S(1)} %bitcast.14, f32[7,2,3584]{2,1,0:T(2,128)} %kappa_hbm.3, bf16[2,7,256,512]{3,2,1,0:T(8,128)(2,1)} %constant.24.clone.table_hbm, s32[1,1024]{1,0:T(1,128)S(1)} %reshape.47.pair_ref), custom_call_target="tpu_custom_call" | custom-call | tf_op jit(solution)/shard_map/synthesise/pallas_call | solution.py:531
  (3 shorter events, 0.0 us)
Async XLA Ops:
  0.0 0.7 copy-start
  8.2 11.7 %copy-start.1 = (s32[896]{0:T(1024)S(1)}, s32[896]{0:T(1024)}, u32[]{:S(2)}) copy-start(s32[896]{0:T(1024)} %param.10) | copy-start | bytes 10756
  8.2 11.8 %copy-start.2 = (s32[896]{0:T(1024)S(1)}, s32[896]{0:T(1024)}, u32[]{:S(2)}) copy-start(s32[896]{0:T(1024)} %param.9) | copy-start | bytes 10756
  8.2 38.5 %all-to-all-start = ((bf16[128,8,896]{2,1,0:T(8,128)(2,1)}), bf16[128,8,896]{2,1,0:T(8,128)(2,1)S(1)}, u32[]{:S(2)}, u32[]{:S(2)}) async-start(bf16[128,8,896]{2,1,0:T(8,128)(2,1)} %bitcast.18), calls=%async_computation | async-start | bytes 3670016 | tf_op jit(solution)/shard_map/all_to_all | solution.py:468
  65.4 31.7 %all-to-all-start.1 = ((bf16[128,8,896]{2,1,0:T(8,128)(2,1)}), bf16[128,8,896]{2,1,0:T(8,128)(2,1)S(1)}, u32[]{:S(2)}, u32[]{:S(2)}) async-start(bf16[128,8,896]{2,1,0:T(8,128)(2,1)} %bitcast.17), calls=%async_computation.1 | async-start | bytes 3670016 | tf_op jit(solution)/shard_map/all_to_all | solution.py:468
